TPU v7x, 32 devices: a whole 2x2x4 slice. The times are simulated.
32 devices in a mesh: row: 4 (over y, x), col: 4 (over z), depth: 2 (over core).
Axes of the slice: x: 2, y: 2, z: 4, core: 2. Of those that a mesh axis runs over, the one named last changes fastest.
Arguments:
- tokens: bfloat16 [512, 8192], P(('col', 'depth'), 'row'), may hold values from -6 to 6
- gate_weight: bfloat16 [8192, 14336], P('row', 'col'), may hold values from -0.0625 to 0.0625
- up_weight: bfloat16 [8192, 14336], P('row', 'col'), may hold values from -0.0625 to 0.0625
- down_weight: bfloat16 [14336, 8192], P('col', 'row'), may hold values from -0.046875 to 0.046875
- cotangent: bfloat16 [512, 8192], P(('col', 'depth'), 'row'), may hold values from -6 to 6
Outputs:
- output: bfloat16 [512, 8192], P(('col', 'depth'), 'row')
- tokens_grad: bfloat16 [512, 8192], P(('col', 'depth'), 'row')
- gate_grad: bfloat16 [8192, 14336], P('row', ('col', 'depth'))
- up_grad: bfloat16 [8192, 14336], P('row', ('col', 'depth'))
- down_grad: bfloat16 [14336, 8192], P(('col', 'depth'), 'row')
All inputs are finite; a program needn't handle non-finite values.
Results may differ from a plain program's by a relative error of at most 0.012.
Values may be sent and summed in bfloat16 or wider, within the bound.
A program may use at most 128 MiB of HBM per device.

v0:
```python
import functools

import jax
import jax.numpy as jnp
from jax import lax
from jax.experimental import pallas as pl
from jax.experimental.pallas import tpu as pltpu
from jax.sharding import PartitionSpec as P

MESH = pl.DeviceIdType.MESH
BF16 = jnp.bfloat16
F32 = jnp.float32


def dot_nn(left, right):
    return jnp.dot(left, right, preferred_element_type=F32)


def dot_nt(left, right):
    return lax.dot_general(
        left, right, (((1,), (1,)), ((), ())), preferred_element_type=F32
    )


def dot_tn(left, right):
    return lax.dot_general(
        left, right, (((0,), (0,)), ((), ())), preferred_element_type=F32
    )


def block(index, size):
    return pl.ds(pl.multiple_of(index * size, size), size)


def kernel(
    dims,
    x_ref, cot_ref, wg_hbm, wu_hbm, wd_hbm,
    out_ref, tg_ref, x_out, cot_out, act_out, dg_out, du_out,
    wg, wu, wd, x_full, cot_full,
    gu_part, gu_recv, d_part, d_recv, gu_own, act, dg, du,
    o_part, o_sib, o_sum, o_recv, t_part, t_sib, t_sum, t_recv,
    w_sem, copy_sem, x_ssem, x_rsem, c_ssem, c_rsem,
    gu_ssem, gu_rsem, d_ssem, d_rsem, act_ssem, act_rsem, h_ssem, h_rsem,
    osib_ssem, osib_rsem, oz_ssem, oz_rsem,
    tsib_ssem, tsib_rsem, tz_ssem, tz_rsem,
):
    n, nz, tl, tr, chunks, ch, parts, pw, sliced = dims
    r = lax.axis_index("row")
    z = lax.axis_index("col")
    d = lax.axis_index("depth")
    half = chunks * ch

    def peer(k):
        return {"row": lax.rem(r + k, n)}

    def zpeer(k):
        return {"col": lax.rem(z + k, nz)}

    sibling = {"depth": 1 - d}

    barrier = pltpu.get_barrier_semaphore()
    for k in range(1, n):
        pl.semaphore_signal(barrier, inc=1, device_id=peer(k), device_id_type=MESH)
    for k in range(1, nz):
        pl.semaphore_signal(barrier, inc=1, device_id=zpeer(k), device_id_type=MESH)
    pl.semaphore_signal(barrier, inc=1, device_id=sibling, device_id_type=MESH)

    if sliced:
        sources = (wg_hbm, wu_hbm, wd_hbm)
    else:
        mine = block(d, half)
        sources = (wg_hbm.at[:, mine], wu_hbm.at[:, mine], wd_hbm.at[mine, :])
    loads = [
        pltpu.make_async_copy(src, dst, w_sem.at[i])
        for i, (src, dst) in enumerate(zip(sources, (wg, wu, wd)))
    ]
    for load in loads:
        load.start()

    def remote(src, dst, ssem, rsem, where):
        return pltpu.make_async_remote_copy(
            src_ref=src, dst_ref=dst, send_sem=ssem, recv_sem=rsem,
            device_id=where, device_id_type=MESH,
        )

    def gather(full, ssem, rsem):
        def hop(zz, way):
            slot = zz * 2 + d
            ref = full.at[block(slot, tl)]
            where = ({"col": z + 1}, {"col": z - 1}, sibling)[way]
            return remote(ref, ref, ssem.at[zz, way], rsem.at[slot], where)

        def arrived(slot):
            ref = full.at[block(slot, tl)]
            remote(ref, ref, ssem.at[0, 0], rsem.at[slot], sibling).wait_recv()

        def first(shard):
            full[block(z * 2 + d, tl), :] = shard[...]

            @pl.when(z + 1 < nz)
            def _():
                hop(z, 0).start()

            @pl.when(z > 0)
            def _():
                hop(z, 1).start()

            hop(z, 2).start()

        def stage(s):
            low, high = z - s, z + s

            @pl.when(low >= 0)
            def _():
                arrived(low * 2 + d)

                @pl.when(z + 1 < nz)
                def _():
                    hop(low, 0).start()

                hop(low, 2).start()

            @pl.when(high < nz)
            def _():
                arrived(high * 2 + d)

                @pl.when(z > 0)
                def _():
                    hop(high, 1).start()

                hop(high, 2).start()

        def last():
            for zz in range(nz):
                arrived(zz * 2 + 1 - d)

        def drain():
            for zz in range(nz):
                @pl.when((zz <= z) & (z + 1 < nz))
                def _():
                    hop(zz, 0).wait_send()

                @pl.when((zz >= z) & (z > 0))
                def _():
                    hop(zz, 1).wait_send()

                hop(zz, 2).wait_send()

        return first, stage, last, drain

    x_first, x_stage, x_last, x_drain = gather(x_full, x_ssem, x_rsem)
    c_first, c_stage, c_last, c_drain = gather(cot_full, c_ssem, c_rsem)

    def gu_copy(c, k):
        rows = block(lax.rem(r + k, n), tr)
        return remote(gu_part.at[c, :, rows, :], gu_recv.at[c, k - 1],
                      gu_ssem.at[c, k - 1], gu_rsem.at[c, k - 1], peer(k))

    def d_copy(c, k):
        rows = block(lax.rem(r + k, n), tr)
        return remote(d_part.at[c, rows, :], d_recv.at[c, k - 1],
                      d_ssem.at[c, k - 1], d_rsem.at[c, k - 1], peer(k))

    mine_rows = block(r, tr)

    def act_copy(c, k, owner=None):
        rows = mine_rows if owner is None else block(owner, tr)
        ref = act.at[rows, block(c, ch)]
        return remote(ref, ref, act_ssem.at[c, k - 1], act_rsem.at[c, k - 1], peer(k))

    def h_copy(which, c, k, owner=None):
        rows = mine_rows if owner is None else block(owner, tr)
        ref = (dg, du)[which].at[rows, block(c, ch)]
        return remote(ref, ref, h_ssem.at[which, c, k - 1], h_rsem.at[which, c, k - 1], peer(k))

    def sender(k):
        return lax.rem(r - k + n, n)

    pl.semaphore_wait(barrier, n - 1 + nz - 1 + 1)

    x_first(x_ref)
    for s in range(1, nz):
        if s == nz - 1:
            c_first(cot_ref)
        x_stage(s)
    x_last()
    if nz == 1:
        c_first(cot_ref)
    x_save = pltpu.make_async_copy(x_full, x_out, copy_sem.at[0])
    x_save.start()

    loads[0].wait()
    loads[1].wait()

    @pl.loop(0, chunks)
    def _(c):
        gu_part[c, 0, :, :] = dot_nn(x_full[...], wg[:, block(c, ch)]).astype(BF16)
        gu_part[c, 1, :, :] = dot_nn(x_full[...], wu[:, block(c, ch)]).astype(BF16)
        for k in range(1, n):
            gu_copy(c, k).start()
        for s in range(1, nz):
            @pl.when(c == min(2 * s - 1, chunks - 1))
            def _():
                c_stage(s)

    c_last()
    cot_save = pltpu.make_async_copy(cot_full, cot_out, copy_sem.at[1])
    cot_save.start()
    loads[2].wait()

    @pl.loop(0, chunks)
    def _(c):
        d_part[c, :, :] = dot_nt(cot_full[...], wd[block(c, ch), :]).astype(BF16)
        for k in range(1, n):
            d_copy(c, k).start()

    @pl.loop(0, chunks)
    def _(c):
        gate = gu_part[c, 0, mine_rows, :].astype(F32)
        up = gu_part[c, 1, mine_rows, :].astype(F32)
        for k in range(1, n):
            gu_copy(c, k).wait_recv()
            gate += gu_recv[c, k - 1, 0].astype(F32)
            up += gu_recv[c, k - 1, 1].astype(F32)
        gu_own[c, 0] = gate
        gu_own[c, 1] = up
        act[mine_rows, block(c, ch)] = (gate * jax.nn.sigmoid(gate) * up).astype(BF16)
        for k in range(1, n):
            act_copy(c, k).start()

    @pl.loop(0, chunks)
    def _(c):
        dact = d_part[c, mine_rows, :].astype(F32)
        for k in range(1, n):
            d_copy(c, k).wait_recv()
            dact += d_recv[c, k - 1].astype(F32)
        gate, up = gu_own[c, 0], gu_own[c, 1]
        sig = jax.nn.sigmoid(gate)
        dg[mine_rows, block(c, ch)] = (
            dact * up * sig * (1.0 + gate * (1.0 - sig))
        ).astype(BF16)
        du[mine_rows, block(c, ch)] = (dact * gate * sig).astype(BF16)
        for k in range(1, n):
            h_copy(0, c, k).start()
            h_copy(1, c, k).start()

    def summing(part, sib, total, recv, sib_ssem, sib_rsem, z_ssem, z_rsem):
        def to_sibling(p):
            cols = block(p, pw)
            return remote(part.at[1 - d, :, :, cols], sib.at[:, :, cols],
                          sib_ssem.at[p], sib_rsem.at[p], sibling)

        def to_col(p, k):
            cols = block(p, pw)
            return remote(total.at[lax.rem(z + k, nz), :, cols], recv.at[k - 1, :, cols],
                          z_ssem.at[p, k - 1], z_rsem.at[p, k - 1], zpeer(k))

        def put(p, value):
            cols = block(p, pw)
            for zz in range(nz):
                for dd in range(2):
                    slot = zz * 2 + dd
                    part[dd, zz, :, cols] = value[slot * tl:(slot + 1) * tl].astype(BF16)
            to_sibling(p).start()

        def spread():
            @pl.loop(0, parts)
            def _(p):
                cols = block(p, pw)
                to_sibling(p).wait_recv()
                total[:, :, cols] = (
                    part[d, :, :, cols].astype(F32) + sib[:, :, cols].astype(F32)
                ).astype(BF16)
                for k in range(1, nz):
                    to_col(p, k).start()

        def finish(result):
            @pl.loop(0, parts)
            def _(p):
                cols = block(p, pw)
                value = total[z, :, cols].astype(F32)
                for k in range(1, nz):
                    to_col(p, k).wait_recv()
                    value += recv[k - 1, :, cols].astype(F32)
                result[:, cols] = value.astype(BF16)

        def drain():
            @pl.loop(0, parts)
            def _(p):
                to_sibling(p).wait_send()
                for k in range(1, nz):
                    to_col(p, k).wait_send()

        return put, spread, finish, drain

    o_put, o_spread, o_finish, o_drain = summing(
        o_part, o_sib, o_sum, o_recv, osib_ssem, osib_rsem, oz_ssem, oz_rsem)
    t_put, t_spread, t_finish, t_drain = summing(
        t_part, t_sib, t_sum, t_recv, tsib_ssem, tsib_rsem, tz_ssem, tz_rsem)

    @pl.loop(0, chunks)
    def _(c):
        for k in range(1, n):
            act_copy(c, k, sender(k)).wait_recv()

    act_save = pltpu.make_async_copy(act, act_out, copy_sem.at[2])
    act_save.start()

    @pl.loop(0, parts)
    def _(p):
        o_put(p, dot_nn(act[...], wd[:, block(p, pw)]))

    o_spread()

    @pl.loop(0, chunks)
    def _(c):
        for k in range(1, n):
            h_copy(0, c, k, sender(k)).wait_recv()
            h_copy(1, c, k, sender(k)).wait_recv()

    dg_save = pltpu.make_async_copy(dg, dg_out, copy_sem.at[3])
    du_save = pltpu.make_async_copy(du, du_out, copy_sem.at[4])
    dg_save.start()
    du_save.start()

    @pl.loop(0, parts)
    def _(p):
        t_put(p, dot_nt(dg[...], wg[block(p, pw), :]) + dot_nt(du[...], wu[block(p, pw), :]))

    t_spread()
    o_finish(out_ref)
    t_finish(tg_ref)

    x_drain()
    c_drain()

    @pl.loop(0, chunks)
    def _(c):
        for k in range(1, n):
            gu_copy(c, k).wait_send()
            d_copy(c, k).wait_send()
            act_copy(c, k).wait_send()
            h_copy(0, c, k).wait_send()
            h_copy(1, c, k).wait_send()

    o_drain()
    t_drain()
    for save in (x_save, cot_save, act_save, dg_save, du_save):
        save.wait()


def group_kernel(
    dims,
    x_ref, cot_ref, wg_hbm, wu_hbm, wd_hbm,
    out_ref, tg_ref, x_out, cot_out, act_out, dg_out, du_out,
    wg, wu, wd, x_full, cot_full, part, recv, h, s_part, s_sib, s_sum, s_recv,
    w_sem, copy_sem, save_sem, x_ssem, x_rsem, c_ssem, c_rsem,
    rs_ssem, rs_rsem, ag_ssem, ag_rsem, sib_ssem, sib_rsem, z_ssem, z_rsem,
):
    nz, tl, half, ch, pw = dims
    feats = x_full.shape[1]
    tg, tr, hs = 2 * tl, tl // 2, half // 2
    r = lax.axis_index("row")
    z = lax.axis_index("col")
    d = lax.axis_index("depth")
    rx = r + 1 - 2 * (r % 2)
    ry = r + 2 - 4 * (r // 2)
    rd = 3 - r
    near, far = (rx, ry), (ry, rx)
    halves = (pl.ds(0, hs), pl.ds(hs, hs))
    sibling = {"depth": 1 - d}
    way = 1 - 2 * (z // max(nz // 2, 1)) if nz > 1 else 1

    barrier = pltpu.get_barrier_semaphore()
    for where in (rx, ry):
        pl.semaphore_signal(barrier, inc=1, device_id={"row": where}, device_id_type=MESH)
    for k in range(1, nz):
        pl.semaphore_signal(barrier, inc=1, device_id={"col": lax.rem(z + k, nz)}, device_id_type=MESH)
    pl.semaphore_signal(barrier, inc=1, device_id=sibling, device_id_type=MESH)

    mine = block(d, half)
    sources = (wg_hbm.at[:, mine], wu_hbm.at[:, mine], wd_hbm.at[mine, :])
    loads = [
        pltpu.make_async_copy(src, dst, w_sem.at[i])
        for i, (src, dst) in enumerate(zip(sources, (wg, wu, wd)))
    ]
    for load in loads:
        load.start()

    def remote(src, dst, ssem, rsem, where):
        return pltpu.make_async_remote_copy(
            src_ref=src, dst_ref=dst, send_sem=ssem, recv_sem=rsem,
            device_id=where, device_id_type=MESH,
        )

    def group(i):
        return lax.rem(z + i * way + nz, nz)

    def gather(full, ssem, rsem):
        def hop(zz, to):
            slot = zz * 2 + d
            ref = full.at[block(slot, tl)]
            where = ({"col": z + 1}, {"col": z - 1}, sibling)[to]
            return remote(ref, ref, ssem.at[zz, to], rsem.at[slot], where)

        def arrived(slot):
            ref = full.at[block(slot, tl)]
            remote(ref, ref, ssem.at[0, 0], rsem.at[slot], sibling).wait_recv()

        def first(shard):
            full[block(z * 2 + d, tl), :] = shard[...]

            @pl.when(z + 1 < nz)
            def _():
                hop(z, 0).start()

            @pl.when(z > 0)
            def _():
                hop(z, 1).start()

            hop(z, 2).start()

        def stage(s):
            low, high = z - s, z + s

            @pl.when(low >= 0)
            def _():
                arrived(low * 2 + d)

                @pl.when(z + 1 < nz)
                def _():
                    hop(low, 0).start()

                hop(low, 2).start()

            @pl.when(high < nz)
            def _():
                arrived(high * 2 + d)

                @pl.when(z > 0)
                def _():
                    hop(high, 1).start()

                hop(high, 2).start()

        def other(g):
            arrived(g * 2 + 1 - d)

        def drain():
            for zz in range(nz):
                @pl.when((zz <= z) & (z + 1 < nz))
                def _():
                    hop(zz, 0).wait_send()

                @pl.when((zz >= z) & (z > 0))
                def _():
                    hop(zz, 1).wait_send()

                hop(zz, 2).wait_send()

        return first, stage, other, drain

    x_first, x_stage, x_other, x_drain = gather(x_full, x_ssem, x_rsem)
    c_first, c_stage, c_other, c_drain = gather(cot_full, c_ssem, c_rsem)

    def rs(i, b, m):
        owner = (rd, near[b], far[b])[m]
        to = far[b] if m == 2 else near[b]
        return remote(part.at[i, :, block(owner, tr), halves[b]],
                      recv.at[i, m, :, :, halves[b]],
                      rs_ssem.at[i, b, m], rs_rsem.at[i, b, m], {"row": to})

    def rows(g, owner):
        return pl.ds(pl.multiple_of(g * tg + owner * tr, tr), tr)

    def ag(i, m, incoming=False):
        g = group(i)
        owner = (rx, ry, rd, rd)[m] if incoming else (r, r, rx, ry)[m]
        ref = h.at[:, rows(g, owner), (pl.ds(0, half), pl.ds(0, half), *halves)[m]]
        to = (rx, ry, ry, rx)[m]
        return remote(ref, ref, ag_ssem.at[i, m], ag_rsem.at[i, m], {"row": to})

    def to_sibling(i):
        g = group(i)
        return remote(s_part.at[g, :, 1 - d], s_sib.at[g], sib_ssem.at[i], sib_rsem.at[i], sibling)

    def to_col(i):
        g = group(i)
        k = lax.rem(z - g + nz, nz) - 1
        return remote(s_sum.at[g], s_recv.at[k], z_ssem.at[i], z_rsem.at[k], {"col": g})

    def saves(i):
        span = block(group(i), tg)
        return [
            pltpu.make_async_copy(h.at[j, span], out.at[span], save_sem.at[i, j])
            for j, out in enumerate((act_out, dg_out, du_out))
        ]

    x_save = pltpu.make_async_copy(x_full, x_out, copy_sem.at[0])
    cot_save = pltpu.make_async_copy(cot_full, cot_out, copy_sem.at[1])

    def compute(i):
        g = group(i)
        span = block(g, tg)

        @pl.when(i > 0)
        def _():
            x_stage(i)
            c_stage(i)

        x_other(g)

        @pl.when(i == 0)
        def _():
            loads[0].wait()
            loads[1].wait()

        @pl.loop(0, half // ch)
        def _(c):
            cols = block(c, ch)
            part[i, 0, :, cols] = dot_nn(x_full[span, :], wg[:, cols]).astype(BF16)
            part[i, 1, :, cols] = dot_nn(x_full[span, :], wu[:, cols]).astype(BF16)

        c_other(g)

        @pl.when(i == 0)
        def _():
            loads[2].wait()

        @pl.loop(0, half // ch)
        def _(c):
            cols = block(c, ch)
            part[i, 2, :, cols] = dot_nt(cot_full[span, :], wd[cols, :]).astype(BF16)

        for m in range(2):
            for b in range(2):
                rs(i, b, m).start()

    def relay(i):
        for b in range(2):
            rs(i, b, 0).wait_recv()
            spot = block(far[b], tr)
            part[i, :, spot, halves[b]] = (
                part[i, :, spot, halves[b]].astype(F32) + recv[i, 0, :, :, halves[b]].astype(F32)
            ).astype(BF16)
            rs(i, b, 2).start()

    def hidden(i):
        g = group(i)
        for b in range(2):
            rs(i, b, 1).wait_recv()
            rs(i, b, 2).wait_recv()
            gate, up, dact = (
                part[i, j, block(r, tr), halves[b]].astype(F32)
                + recv[i, 1, j, :, halves[b]].astype(F32)
                + recv[i, 2, j, :, halves[b]].astype(F32)
                for j in range(3)
            )
            sig = jax.nn.sigmoid(gate)
            own = rows(g, r)
            h[0, own, halves[b]] = (gate * sig * up).astype(BF16)
            h[1, own, halves[b]] = (dact * up * sig * (1.0 + gate * (1.0 - sig))).astype(BF16)
            h[2, own, halves[b]] = (dact * gate * sig).astype(BF16)
        ag(i, 0).start()
        ag(i, 1).start()

    def forward(i):
        for m in range(2):
            ag(i, m, True).wait_recv()
            ag(i, m + 2).start()

    def project(i):
        g = group(i)
        span = block(g, tg)
        ag(i, 2, True).wait_recv()
        ag(i, 3, True).wait_recv()
        for save in saves(i):
            save.start()

        @pl.loop(0, feats // pw)
        def _(p):
            cols = block(p, pw)
            out = dot_nn(h[0, span, :], wd[:, cols]).astype(BF16)
            grad = (dot_nt(h[1, span, :], wg[cols, :]) + dot_nt(h[2, span, :], wu[cols, :])).astype(BF16)
            for dd in range(2):
                s_part[g, 0, dd, :, cols] = out[dd * tl:(dd + 1) * tl]
                s_part[g, 1, dd, :, cols] = grad[dd * tl:(dd + 1) * tl]

        to_sibling(i).start()

    def spread(i):
        g = group(i)
        to_sibling(i).wait_recv()
        for j in range(2):
            s_sum[g, j] = (s_part[g, j, d].astype(F32) + s_sib[g, j].astype(F32)).astype(BF16)

        @pl.when(i > 0)
        def _():
            to_col(i).start()

    pl.semaphore_wait(barrier, 2 + nz - 1 + 1)
    x_first(x_ref)
    c_first(cot_ref)

    @pl.loop(0, nz + 2)
    def _(t):
        now, before, last = t < nz, (t >= 1) & (t <= nz), t >= 2

        @pl.when(now)
        def _():
            compute(t)

        @pl.when(t == nz - 1)
        def _():
            x_save.start()
            cot_save.start()

        @pl.when(before)
        def _():
            hidden(t - 1)

        @pl.when(last)
        def _():
            project(t - 2)

        @pl.when(now)
        def _():
            relay(t)

        @pl.when(before)
        def _():
            forward(t - 1)

        @pl.when(last)
        def _():
            spread(t - 2)

    def landed(k):
        remote(s_sum.at[0], s_recv.at[k], z_ssem.at[0], z_rsem.at[k], sibling).wait_recv()

    for k in range(nz - 1):
        landed(k)
    for j, result in enumerate((out_ref, tg_ref)):
        value = s_sum[z, j].astype(F32)
        for k in range(nz - 1):
            value += s_recv[k, j].astype(F32)
        result[...] = value.astype(BF16)

    x_drain()
    c_drain()

    @pl.loop(0, nz)
    def _(i):
        for b in range(2):
            for m in range(3):
                rs(i, b, m).wait_send()
        for m in range(4):
            ag(i, m).wait_send()
        to_sibling(i).wait_send()

        @pl.when(i > 0)
        def _():
            to_col(i).wait_send()

        for save in saves(i):
            save.wait()

    x_save.wait()
    cot_save.wait()


def per_device(n, nz, tokens, gate_weight, up_weight, down_weight, cotangent):
    tl, feats = tokens.shape
    half = gate_weight.shape[1] // 2
    total = tl * nz * 2
    tr = total // n
    ch = 256 if half % 256 == 0 else half
    chunks = half // ch
    pw = 512 if feats % 512 == 0 else feats
    parts = feats // pw
    sliced = half % 128 != 0
    if sliced:
        start = lax.axis_index("depth") * half
        weights = (
            lax.dynamic_slice_in_dim(gate_weight, start, half, 1),
            lax.dynamic_slice_in_dim(up_weight, start, half, 1),
            lax.dynamic_slice_in_dim(down_weight, start, half, 0),
        )
    else:
        weights = (gate_weight, up_weight, down_weight)

    def sds(*shape):
        return jax.ShapeDtypeStruct(shape, BF16)

    def buf(*shape):
        return pltpu.VMEM(shape, BF16)

    def sem(*shape):
        return pltpu.SemaphoreType.DMA(shape)

    vmem = pl.BlockSpec(memory_space=pltpu.VMEM)
    hbm = pl.BlockSpec(memory_space=pl.ANY)
    if n == 4 and nz % 2 == 0 and tl % 32 == 0 and half % 256 == 0:
        output, tokens_grad, x_both, cot_both, act, dgate, dup = pl.pallas_call(
            functools.partial(group_kernel, (nz, tl, half, half // 2, 2 * pw if parts % 2 == 0 else pw)),
            out_shape=(
                sds(tl, feats), sds(tl, feats), sds(total, feats), sds(total, feats),
                sds(total, half), sds(total, half), sds(total, half),
            ),
            in_specs=[vmem, vmem, hbm, hbm, hbm],
            out_specs=(vmem, vmem, hbm, hbm, hbm, hbm, hbm),
            scratch_shapes=[
                buf(feats, half), buf(feats, half), buf(half, feats),
                buf(total, feats), buf(total, feats),
                buf(nz, 3, 2 * tl, half), buf(nz, 3, 3, tl // 2, half),
                buf(3, total, half),
                buf(nz, 2, 2, tl, feats), buf(nz, 2, tl, feats), buf(nz, 2, tl, feats),
                buf(max(nz - 1, 1), 2, tl, feats),
                sem(3), sem(2), sem(nz, 3),
                sem(nz, 3), sem(nz * 2), sem(nz, 3), sem(nz * 2),
                sem(nz, 2, 3), sem(nz, 2, 3), sem(nz, 4), sem(nz, 4),
                sem(nz), sem(nz), sem(nz), sem(nz),
            ],
            compiler_params=pltpu.CompilerParams(
                collective_id=1, has_side_effects=True, vmem_limit_bytes=60 * 2**20
            ),
            cost_estimate=pl.CostEstimate(
                flops=12 * total * feats * half, bytes_accessed=8 * feats * half,
                transcendentals=0,
            ),
        )(tokens, cotangent, *weights)
    else:
        sums = [
            buf(2, nz, tl, feats), buf(nz, tl, feats), buf(nz, tl, feats),
            buf(max(nz - 1, 1), tl, feats),
        ]
        sum_sems = [sem(parts), sem(parts), sem(parts, nz), sem(parts, nz)]
        output, tokens_grad, x_both, cot_both, act, dgate, dup = pl.pallas_call(
            functools.partial(kernel, (n, nz, tl, tr, chunks, ch, parts, pw, sliced)),
            out_shape=(
                sds(tl, feats), sds(tl, feats), sds(total, feats), sds(total, feats),
                sds(total, half), sds(total, half), sds(total, half),
            ),
            in_specs=[vmem, vmem, hbm, hbm, hbm],
            out_specs=(vmem, vmem, hbm, hbm, hbm, hbm, hbm),
            scratch_shapes=[
                buf(feats, half), buf(feats, half), buf(half, feats),
                buf(total, feats), buf(total, feats),
                buf(chunks, 2, total, ch), buf(chunks, n - 1, 2, tr, ch),
                buf(chunks, total, ch), buf(chunks, n - 1, tr, ch),
                pltpu.VMEM((chunks, 2, tr, ch), F32),
                buf(total, half), buf(total, half), buf(total, half),
                *sums, *sums,
                sem(3), sem(5),
                sem(nz, 3), sem(nz * 2), sem(nz, 3), sem(nz * 2),
                sem(chunks, n - 1), sem(chunks, n - 1),
                sem(chunks, n - 1), sem(chunks, n - 1),
                sem(chunks, n - 1), sem(chunks, n - 1),
                sem(2, chunks, n - 1), sem(2, chunks, n - 1),
                *sum_sems, *sum_sems,
            ],
            compiler_params=pltpu.CompilerParams(
                collective_id=0, has_side_effects=True, vmem_limit_bytes=60 * 2**20
            ),
            cost_estimate=pl.CostEstimate(
                flops=12 * total * feats * half, bytes_accessed=8 * feats * half,
                transcendentals=0,
            ),
        )(tokens, cotangent, *weights)
    gate_grad = dot_tn(x_both, dgate)
    up_grad = dot_tn(x_both, dup)
    down_grad = dot_tn(act, cot_both)
    return (
        output,
        tokens_grad,
        gate_grad.astype(BF16),
        up_grad.astype(BF16),
        down_grad.astype(BF16),
    )


def solution(mesh):
    return jax.shard_map(
        functools.partial(per_device, mesh.shape["row"], mesh.shape["col"]),
        mesh=mesh,
        in_specs=(
            P(("col", "depth"), "row"),
            P("row", "col"),
            P("row", "col"),
            P("col", "row"),
            P(("col", "depth"), "row"),
        ),
        out_specs=(
            P(("col", "depth"), "row"),
            P(("col", "depth"), "row"),
            P("row", ("col", "depth")),
            P("row", ("col", "depth")),
            P(("col", "depth"), "row"),
        ),
        check_vma=False,
    )
```

profile of v0, /device:TPU:0, one launch (start us, length us, event | category | flops | bytes accessed | tf_op | source)
XLA Modules:
  0.0 174.4 jit_solution(5529461847223986827)
XLA Ops:
  0.6 150.7 %shard_map.92 = (bf16[64,2048]{1,0:T(8,128)(2,1)}, bf16[64,2048]{1,0:T(8,128)(2,1)}, bf16[512,2048]{1,0:T(8,128)(2,1)}, bf16[512,2048]{1,0:T(8,128)(2,1)}, bf16[...) custom-call(bf16[64,2048]{1,0:T(8,128)(2,1)} %x_ref.1, bf16[64,2048]{1,0:T(8,128)(2,1)} %cot_ref.1, ...), custom_call_target="tpu_custom_call" | custom-call | flops 22548578304 | bytes 29360128 | tf_op jit(solution)/shard_map/pallas_call | solution.py:704
  151.4 0.0 copy-start.3
  151.4 0.0 copy-start.5
  151.4 9.4 %convolution_convert_fusion.2 = bf16[2048,1792]{1,0:T(8,128)(2,1)} fusion(bf16[512,2048]{1,0:T(8,128)(2,1)} %get-tuple-element.14, bf16[512,1792]{1,0:T(8,128)(2,1)} %get-tuple-element.15), kind=kOutput, calls=%fused_computation.2 | convolution fusion | flops 3761766400 | bytes 11272192 | tf_op jit(solution)/shard_map/dot_general | solution.py:26
  160.7 0.0 copy-done.3
  160.7 0.0 copy-done.5
  160.7 0.0 copy-start.2
  160.7 0.0 copy-start.4
  160.8 6.1 %convolution_convert_fusion.1 = bf16[2048,1792]{1,0:T(8,128)(2,1)} fusion(bf16[512,2048]{1,0:T(8,128)(2,1)S(1)} %copy-done.3, bf16[512,1792]{1,0:T(8,128)(2,1)S(1)} %copy-done.5), kind=kOutput, calls=%fused_computation.1 | convolution fusion | flops 3761766400 | bytes 11272192 | tf_op jit(solution)/shard_map/dot_general | solution.py:26
  166.9 0.0 copy-done.2
  166.9 0.0 copy-done.4
  166.9 0.0 copy-start.1
  166.9 0.0 copy-start
  166.9 6.1 %convolution_convert_fusion = bf16[1792,2048]{1,0:T(8,128)(2,1)} fusion(bf16[512,1792]{1,0:T(8,128)(2,1)S(1)} %copy-done.4, bf16[512,2048]{1,0:T(8,128)(2,1)S(1)} %copy-done.2), kind=kOutput, calls=%fused_computation | convolution fusion | flops 3761766400 | bytes 11272192 | tf_op jit(solution)/shard_map/dot_general | solution.py:26
  173.0 0.0 copy-done.1
  173.0 0.7 copy.12
  173.7 0.0 copy-done
  173.7 0.7 copy.13
Async XLA Ops:
  151.4 9.4 %copy-start.3 = (bf16[512,2048]{1,0:T(8,128)(2,1)S(1)}, bf16[512,2048]{1,0:T(8,128)(2,1)}, u32[]{:S(2)}) copy-start(bf16[512,2048]{1,0:T(8,128)(2,1)} %get-tuple-element.14) | copy-start | bytes 6291460
  151.4 9.4 %copy-start.5 = (bf16[512,1792]{1,0:T(8,128)(2,1)S(1)}, bf16[512,1792]{1,0:T(8,128)(2,1)}, u32[]{:S(2)}) copy-start(bf16[512,1792]{1,0:T(8,128)(2,1)} %get-tuple-element.16) | copy-start | bytes 5505028
  160.7 6.1 %copy-start.2 = (bf16[512,2048]{1,0:T(8,128)(2,1)S(1)}, bf16[512,2048]{1,0:T(8,128)(2,1)}, u32[]{:S(2)}) copy-start(bf16[512,2048]{1,0:T(8,128)(2,1)} %get-tuple-element.18) | copy-start | bytes 6291460
  160.7 6.1 %copy-start.4 = (bf16[512,1792]{1,0:T(8,128)(2,1)S(1)}, bf16[512,1792]{1,0:T(8,128)(2,1)}, u32[]{:S(2)}) copy-start(bf16[512,1792]{1,0:T(8,128)(2,1)} %get-tuple-element.17) | copy-start | bytes 5505028
  166.9 6.1 %copy-start.1 = (bf16[64,2048]{1,0:T(8,128)(2,1)S(1)}, bf16[64,2048]{1,0:T(8,128)(2,1)}, u32[]{:S(2)}) copy-start(bf16[64,2048]{1,0:T(8,128)(2,1)} %get-tuple-element.24) | copy-start | bytes 786436
  166.9 6.8 %copy-start = (bf16[64,2048]{1,0:T(8,128)(2,1)S(1)}, bf16[64,2048]{1,0:T(8,128)(2,1)}, u32[]{:S(2)}) copy-start(bf16[64,2048]{1,0:T(8,128)(2,1)} %get-tuple-element.25) | copy-start | bytes 786436
where the time goes:
time: 175 us; the launch traced here: 174 us
  Pallas kernels  151 us (86%)
  matrix products  21.6 us (12%)
    pallas_call x1, Pallas kernels, per_device(): pl.pallas_call(functools.partial(group_kernel, (nz, tl, half, half // 2,...  151 us
    dot_general x3, matrix products, dot_tn(): lax.dot_general(left, right, (((0,), (0,)), ((), ())), preferred_element_...  21.6 us

commit v1 on v0

--- a/solution.py
+++ b/solution.py
@@ -353,23 +353,25 @@
     dims,
     x_ref, cot_ref, wg_hbm, wu_hbm, wd_hbm,
     out_ref, tg_ref, x_out, cot_out, act_out, dg_out, du_out,
-    wg, wu, wd, x_full, cot_full, part, recv, h, s_part, s_sib, s_sum, s_recv,
+    wg, wu, wd, x_full, cot_full, part, recv, h, acc, s_part, s_sib, s_sum, s_recv,
     w_sem, copy_sem, save_sem, x_ssem, x_rsem, c_ssem, c_rsem,
     rs_ssem, rs_rsem, ag_ssem, ag_rsem, sib_ssem, sib_rsem, z_ssem, z_rsem,
 ):
-    nz, tl, half, ch, pw = dims
+    nz, tl, half, pw = dims
     feats = x_full.shape[1]
-    tg, tr, hs = 2 * tl, tl // 2, half // 2
+    tg, tr, hw = 2 * tl, tl // 2, half // 2
+    units = 2 * nz
+    wide = (hw // 2 + 127) // 128 * 128
+    widths = (wide, hw - wide)
+    starts = (0, wide)
     r = lax.axis_index("row")
     z = lax.axis_index("col")
     d = lax.axis_index("depth")
     rx = r + 1 - 2 * (r % 2)
     ry = r + 2 - 4 * (r // 2)
     rd = 3 - r
-    near, far = (rx, ry), (ry, rx)
-    halves = (pl.ds(0, hs), pl.ds(hs, hs))
     sibling = {"depth": 1 - d}
-    way = 1 - 2 * (z // max(nz // 2, 1)) if nz > 1 else 1
+    way = 1 - 2 * (z // max(nz // 2, 1))
 
     barrier = pltpu.get_barrier_semaphore()
     for where in (rx, ry):
@@ -378,14 +380,18 @@
         pl.semaphore_signal(barrier, inc=1, device_id={"col": lax.rem(z + k, nz)}, device_id_type=MESH)
     pl.semaphore_signal(barrier, inc=1, device_id=sibling, device_id_type=MESH)
 
-    mine = block(d, half)
-    sources = (wg_hbm.at[:, mine], wu_hbm.at[:, mine], wd_hbm.at[mine, :])
-    loads = [
-        pltpu.make_async_copy(src, dst, w_sem.at[i])
-        for i, (src, dst) in enumerate(zip(sources, (wg, wu, wd)))
-    ]
-    for load in loads:
-        load.start()
+    def load(i, s):
+        here = pl.ds(s * hw, hw)
+        there = block(2 * d + s, hw)
+        src, dst = (
+            (wg_hbm.at[:, there], wg.at[:, here]),
+            (wu_hbm.at[:, there], wu.at[:, here]),
+            (wd_hbm.at[there, :], wd.at[here, :]),
+        )[i]
+        return pltpu.make_async_copy(src, dst, w_sem.at[i, s])
+
+    for i in range(3):
+        load(i, 0).start()
 
     def remote(src, dst, ssem, rsem, where):
         return pltpu.make_async_remote_copy(
@@ -393,8 +399,21 @@
             device_id=where, device_id_type=MESH,
         )
 
+    def index(u):
+        return lax.rem((u + 1) // 2, nz)
+
+    def side(u):
+        return lax.rem(u + 1 + (index(u) == 0).astype(jnp.int32), 2)
+
     def group(i):
         return lax.rem(z + i * way + nz, nz)
+
+    def ends(u):
+        flip = lax.rem(u, 2)
+        return rx + flip * (ry - rx), ry + flip * (rx - ry)
+
+    def span_of(u, b):
+        return pl.ds(pl.multiple_of(side(u) * hw + starts[b], 128), widths[b])
 
     def gather(full, ssem, rsem):
         def hop(zz, to):
@@ -409,6 +428,7 @@
 
         def first(shard):
             full[block(z * 2 + d, tl), :] = shard[...]
+            hop(z, 2).start()
 
             @pl.when(z + 1 < nz)
             def _():
@@ -417,8 +437,6 @@
             @pl.when(z > 0)
             def _():
                 hop(z, 1).start()
-
-            hop(z, 2).start()
 
         def stage(s):
             low, high = z - s, z + s
@@ -463,22 +481,27 @@
     x_first, x_stage, x_other, x_drain = gather(x_full, x_ssem, x_rsem)
     c_first, c_stage, c_other, c_drain = gather(cot_full, c_ssem, c_rsem)
 
-    def rs(i, b, m):
-        owner = (rd, near[b], far[b])[m]
-        to = far[b] if m == 2 else near[b]
-        return remote(part.at[i, :, block(owner, tr), halves[b]],
-                      recv.at[i, m, :, :, halves[b]],
-                      rs_ssem.at[i, b, m], rs_rsem.at[i, b, m], {"row": to})
+    def rs(u, b, m):
+        i = index(u)
+        near, far = ends(u) if b == 0 else ends(u)[::-1]
+        owner = (rd, near, far)[m]
+        to = far if m == 2 else near
+        cols = span_of(u, b)
+        return remote(part.at[i, :, block(owner, tr), cols],
+                      recv.at[i, m, :, :, cols],
+                      rs_ssem.at[u, b, m], rs_rsem.at[u, b, m], {"row": to})
 
     def rows(g, owner):
         return pl.ds(pl.multiple_of(g * tg + owner * tr, tr), tr)
 
-    def ag(i, m, incoming=False):
-        g = group(i)
-        owner = (rx, ry, rd, rd)[m] if incoming else (r, r, rx, ry)[m]
-        ref = h.at[:, rows(g, owner), (pl.ds(0, half), pl.ds(0, half), *halves)[m]]
-        to = (rx, ry, ry, rx)[m]
-        return remote(ref, ref, ag_ssem.at[i, m], ag_rsem.at[i, m], {"row": to})
+    def ag(u, m, incoming=False):
+        g = group(index(u))
+        p, q = ends(u)
+        owner = (p, q, rd, rd)[m] if incoming else (r, r, p, q)[m]
+        cols = block(side(u), hw) if m < 2 else span_of(u, m - 2)
+        ref = h.at[:, rows(g, owner), cols]
+        to = (p, q, q, p)[m]
+        return remote(ref, ref, ag_ssem.at[u, m], ag_rsem.at[u, m], {"row": to})
 
     def to_sibling(i):
         g = group(i)
@@ -489,151 +512,176 @@
         k = lax.rem(z - g + nz, nz) - 1
         return remote(s_sum.at[g], s_recv.at[k], z_ssem.at[i], z_rsem.at[k], {"col": g})
 
-    def saves(i):
-        span = block(group(i), tg)
+    def saves(u):
+        span, cols = block(group(index(u)), tg), block(side(u), hw)
         return [
-            pltpu.make_async_copy(h.at[j, span], out.at[span], save_sem.at[i, j])
+            pltpu.make_async_copy(h.at[j, span, cols], out.at[span, cols], save_sem.at[u, j])
             for j, out in enumerate((act_out, dg_out, du_out))
         ]
 
     x_save = pltpu.make_async_copy(x_full, x_out, copy_sem.at[0])
     cot_save = pltpu.make_async_copy(cot_full, cot_out, copy_sem.at[1])
 
-    def compute(i):
+    def compute(u):
+        i = index(u)
         g = group(i)
         span = block(g, tg)
-
-        @pl.when(i > 0)
-        def _():
-            x_stage(i)
-            c_stage(i)
-
-        x_other(g)
-
-        @pl.when(i == 0)
-        def _():
-            loads[0].wait()
-            loads[1].wait()
-
-        @pl.loop(0, half // ch)
-        def _(c):
-            cols = block(c, ch)
-            part[i, 0, :, cols] = dot_nn(x_full[span, :], wg[:, cols]).astype(BF16)
-            part[i, 1, :, cols] = dot_nn(x_full[span, :], wu[:, cols]).astype(BF16)
-
-        c_other(g)
-
-        @pl.when(i == 0)
-        def _():
-            loads[2].wait()
-
-        @pl.loop(0, half // ch)
-        def _(c):
-            cols = block(c, ch)
-            part[i, 2, :, cols] = dot_nt(cot_full[span, :], wd[cols, :]).astype(BF16)
+        cols = block(side(u), hw)
+        opens = (u == 0) | ((i > 0) & (lax.rem(u, 2) == 1))
+
+        @pl.when((u > 0) & (u < nz))
+        def _():
+            x_stage(u)
+            c_stage(u)
+
+        @pl.when(opens)
+        def _():
+            x_other(g)
+
+        @pl.when(u == 0)
+        def _():
+            load(0, 0).wait()
+            load(1, 0).wait()
+
+        @pl.when(u == 1)
+        def _():
+            for k in range(3):
+                load(k, 1).wait()
+
+        part[i, 0, :, cols] = dot_nn(x_full[span, :], wg[:, cols]).astype(BF16)
+        part[i, 1, :, cols] = dot_nn(x_full[span, :], wu[:, cols]).astype(BF16)
+
+        @pl.when(opens)
+        def _():
+            c_other(g)
+
+        @pl.when(u == 0)
+        def _():
+            load(2, 0).wait()
+            for k in range(3):
+                load(k, 1).start()
+
+        part[i, 2, :, cols] = dot_nt(cot_full[span, :], wd[cols, :]).astype(BF16)
 
         for m in range(2):
             for b in range(2):
-                rs(i, b, m).start()
-
-    def relay(i):
+                rs(u, b, m).start()
+
+    def relay(u):
+        i = index(u)
         for b in range(2):
-            rs(i, b, 0).wait_recv()
-            spot = block(far[b], tr)
-            part[i, :, spot, halves[b]] = (
-                part[i, :, spot, halves[b]].astype(F32) + recv[i, 0, :, :, halves[b]].astype(F32)
+            rs(u, b, 0).wait_recv()
+            spot, cols = block(ends(u)[1 - b], tr), span_of(u, b)
+            part[i, :, spot, cols] = (
+                part[i, :, spot, cols].astype(F32) + recv[i, 0, :, :, cols].astype(F32)
             ).astype(BF16)
-            rs(i, b, 2).start()
-
-    def hidden(i):
-        g = group(i)
+            rs(u, b, 2).start()
+
+    def hidden(u):
+        i = index(u)
+        own = rows(group(i), r)
         for b in range(2):
-            rs(i, b, 1).wait_recv()
-            rs(i, b, 2).wait_recv()
+            rs(u, b, 1).wait_recv()
+            rs(u, b, 2).wait_recv()
+            cols = span_of(u, b)
             gate, up, dact = (
-                part[i, j, block(r, tr), halves[b]].astype(F32)
-                + recv[i, 1, j, :, halves[b]].astype(F32)
-                + recv[i, 2, j, :, halves[b]].astype(F32)
+                part[i, j, block(r, tr), cols].astype(F32)
+                + recv[i, 1, j, :, cols].astype(F32)
+                + recv[i, 2, j, :, cols].astype(F32)
                 for j in range(3)
             )
             sig = jax.nn.sigmoid(gate)
-            own = rows(g, r)
-            h[0, own, halves[b]] = (gate * sig * up).astype(BF16)
-            h[1, own, halves[b]] = (dact * up * sig * (1.0 + gate * (1.0 - sig))).astype(BF16)
-            h[2, own, halves[b]] = (dact * gate * sig).astype(BF16)
-        ag(i, 0).start()
-        ag(i, 1).start()
-
-    def forward(i):
+            h[0, own, cols] = (gate * sig * up).astype(BF16)
+            h[1, own, cols] = (dact * up * sig * (1.0 + gate * (1.0 - sig))).astype(BF16)
+            h[2, own, cols] = (dact * gate * sig).astype(BF16)
+        ag(u, 0).start()
+        ag(u, 1).start()
+
+    def forward(u):
         for m in range(2):
-            ag(i, m, True).wait_recv()
-            ag(i, m + 2).start()
-
-    def project(i):
+            ag(u, m, True).wait_recv()
+            ag(u, m + 2).start()
+
+    def project(u):
+        i = index(u)
         g = group(i)
-        span = block(g, tg)
-        ag(i, 2, True).wait_recv()
-        ag(i, 3, True).wait_recv()
-        for save in saves(i):
+        span, hid = block(g, tg), block(side(u), hw)
+        slot = jnp.minimum(i, 1)
+        opens = (u == 0) | ((i > 0) & (lax.rem(u, 2) == 1))
+        ag(u, 2, True).wait_recv()
+        ag(u, 3, True).wait_recv()
+        for save in saves(u):
             save.start()
 
-        @pl.loop(0, feats // pw)
-        def _(p):
-            cols = block(p, pw)
-            out = dot_nn(h[0, span, :], wd[:, cols]).astype(BF16)
-            grad = (dot_nt(h[1, span, :], wg[cols, :]) + dot_nt(h[2, span, :], wu[cols, :])).astype(BF16)
-            for dd in range(2):
-                s_part[g, 0, dd, :, cols] = out[dd * tl:(dd + 1) * tl]
-                s_part[g, 1, dd, :, cols] = grad[dd * tl:(dd + 1) * tl]
-
-        to_sibling(i).start()
+        def products(cols):
+            out = dot_nn(h[0, span, hid], wd[hid, cols])
+            grad = dot_nt(h[1, span, hid], wg[cols, hid]) + dot_nt(h[2, span, hid], wu[cols, hid])
+            return out, grad
+
+        @pl.when(opens)
+        def _():
+            @pl.loop(0, feats // pw)
+            def _(p):
+                cols = block(p, pw)
+                out, grad = products(cols)
+                acc[slot, 0, :, cols] = out
+                acc[slot, 1, :, cols] = grad
+
+        @pl.when(jnp.logical_not(opens))
+        def _():
+            @pl.loop(0, feats // pw)
+            def _(p):
+                cols = block(p, pw)
+                for j, value in enumerate(products(cols)):
+                    value = (value + acc[slot, j, :, cols]).astype(BF16)
+                    for dd in range(2):
+                        s_part[g, j, dd, :, cols] = value[dd * tl:(dd + 1) * tl]
+
+            to_sibling(i).start()
 
     def spread(i):
         g = group(i)
         to_sibling(i).wait_recv()
         for j in range(2):
             s_sum[g, j] = (s_part[g, j, d].astype(F32) + s_sib[g, j].astype(F32)).astype(BF16)
-
-        @pl.when(i > 0)
-        def _():
-            to_col(i).start()
+        to_col(i).start()
 
     pl.semaphore_wait(barrier, 2 + nz - 1 + 1)
     x_first(x_ref)
     c_first(cot_ref)
 
-    @pl.loop(0, nz + 2)
+    @pl.loop(0, units + 3)
     def _(t):
-        now, before, last = t < nz, (t >= 1) & (t <= nz), t >= 2
-
-        @pl.when(now)
+        @pl.when(t < units)
         def _():
             compute(t)
 
-        @pl.when(t == nz - 1)
+        @pl.when(t == units - 2)
         def _():
             x_save.start()
             cot_save.start()
 
-        @pl.when(before)
+        @pl.when((t >= 2) & (t < units + 2))
+        def _():
+            forward(t - 2)
+
+        @pl.when((t >= 1) & (t < units + 1))
         def _():
             hidden(t - 1)
 
-        @pl.when(last)
-        def _():
-            project(t - 2)
-
-        @pl.when(now)
+        @pl.when(t >= 3)
+        def _():
+            project(t - 3)
+
+        @pl.when(t < units)
         def _():
             relay(t)
 
-        @pl.when(before)
-        def _():
-            forward(t - 1)
-
-        @pl.when(last)
-        def _():
-            spread(t - 2)
+        @pl.when((t >= 5) & (t < units + 2) & (lax.rem(t, 2) == 1))
+        def _():
+            spread((t - 3) // 2)
+
+    to_sibling(0).wait_recv()
 
     def landed(k):
         remote(s_sum.at[0], s_recv.at[k], z_ssem.at[0], z_rsem.at[k], sibling).wait_recv()
@@ -641,7 +689,7 @@
     for k in range(nz - 1):
         landed(k)
     for j, result in enumerate((out_ref, tg_ref)):
-        value = s_sum[z, j].astype(F32)
+        value = s_part[z, j, d].astype(F32) + s_sib[z, j].astype(F32)
         for k in range(nz - 1):
             value += s_recv[k, j].astype(F32)
         result[...] = value.astype(BF16)
@@ -649,21 +697,23 @@
     x_drain()
     c_drain()
 
+    @pl.loop(0, units)
+    def _(u):
+        for b in range(2):
+            for m in range(3):
+                rs(u, b, m).wait_send()
+        for m in range(4):
+            ag(u, m).wait_send()
+        for save in saves(u):
+            save.wait()
+
     @pl.loop(0, nz)
     def _(i):
-        for b in range(2):
-            for m in range(3):
-                rs(i, b, m).wait_send()
-        for m in range(4):
-            ag(i, m).wait_send()
         to_sibling(i).wait_send()
 
         @pl.when(i > 0)
         def _():
             to_col(i).wait_send()
-
-        for save in saves(i):
-            save.wait()
 
     x_save.wait()
     cot_save.wait()
@@ -700,9 +750,9 @@
 
     vmem = pl.BlockSpec(memory_space=pltpu.VMEM)
     hbm = pl.BlockSpec(memory_space=pl.ANY)
-    if n == 4 and nz % 2 == 0 and tl % 32 == 0 and half % 256 == 0:
+    if n == 4 and nz % 2 == 0 and tl % 32 == 0 and half % 256 == 0 and half >= 512:
         output, tokens_grad, x_both, cot_both, act, dgate, dup = pl.pallas_call(
-            functools.partial(group_kernel, (nz, tl, half, half // 2, 2 * pw if parts % 2 == 0 else pw)),
+            functools.partial(group_kernel, (nz, tl, half, 2 * pw if parts % 2 == 0 else pw)),
             out_shape=(
                 sds(tl, feats), sds(tl, feats), sds(total, feats), sds(total, feats),
                 sds(total, half), sds(total, half), sds(total, half),
@@ -713,12 +763,12 @@
                 buf(feats, half), buf(feats, half), buf(half, feats),
                 buf(total, feats), buf(total, feats),
                 buf(nz, 3, 2 * tl, half), buf(nz, 3, 3, tl // 2, half),
-                buf(3, total, half),
+                buf(3, total, half), pltpu.VMEM((2, 2, 2 * tl, feats), F32),
                 buf(nz, 2, 2, tl, feats), buf(nz, 2, tl, feats), buf(nz, 2, tl, feats),
                 buf(max(nz - 1, 1), 2, tl, feats),
-                sem(3), sem(2), sem(nz, 3),
+                sem(3, 2), sem(2), sem(2 * nz, 3),
                 sem(nz, 3), sem(nz * 2), sem(nz, 3), sem(nz * 2),
-                sem(nz, 2, 3), sem(nz, 2, 3), sem(nz, 4), sem(nz, 4),
+                sem(2 * nz, 2, 3), sem(2 * nz, 2, 3), sem(2 * nz, 4), sem(2 * nz, 4),
                 sem(nz), sem(nz), sem(nz), sem(nz),
             ],
             compiler_params=pltpu.CompilerParams(

time: 175 us -> 169 us (0.966)
  Pallas kernels: 151 us -> 145 us
    pallas_call x1, Pallas kernels: 151 us -> 145 us  [per_device(): pl.pallas_call(functools.partial(group_kernel, (nz, tl, half, 2 * pw if p...]
where the time goes in v1:
time: 169 us
  Pallas kernels  145 us (86%)
  matrix products  21.6 us (13%)
    pallas_call x1, Pallas kernels, per_device(): pl.pallas_call(functools.partial(group_kernel, (nz, tl, half, 2 * pw if p...  145 us
    dot_general x3, matrix products, dot_tn(): lax.dot_general(left, right, (((0,), (0,)), ((), ())), preferred_element_...  21.6 us

profile of v1, /device:TPU:0, one launch (start us, length us, event | category | flops | bytes accessed | tf_op | source)
XLA Modules:
  0.0 168.7 jit_solution(13572870824811628052)
XLA Ops:
  0.6 145.0 %shard_map.92 = (bf16[64,2048]{1,0:T(8,128)(2,1)}, bf16[64,2048]{1,0:T(8,128)(2,1)}, bf16[512,2048]{1,0:T(8,128)(2,1)}, bf16[512,2048]{1,0:T(8,128)(2,1)}, bf16[...) custom-call(bf16[64,2048]{1,0:T(8,128)(2,1)} %x_ref.1, bf16[64,2048]{1,0:T(8,128)(2,1)} %cot_ref.1, ...), custom_call_target="tpu_custom_call" | custom-call | flops 22548578304 | bytes 29360128 | tf_op jit(solution)/shard_map/pallas_call | solution.py:754
  145.7 0.0 copy-start.3
  145.7 0.0 copy-start.5
  145.7 9.4 %convolution_convert_fusion.2 = bf16[2048,1792]{1,0:T(8,128)(2,1)} fusion(bf16[512,2048]{1,0:T(8,128)(2,1)} %get-tuple-element.14, bf16[512,1792]{1,0:T(8,128)(2,1)} %get-tuple-element.15), kind=kOutput, calls=%fused_computation.2 | convolution fusion | flops 3761766400 | bytes 11272192 | tf_op jit(solution)/shard_map/dot_general | solution.py:26
  155.0 0.0 copy-done.3
  155.1 0.0 copy-done.5
  155.1 0.0 copy-start.2
  155.1 0.0 copy-start.4
  155.1 6.1 %convolution_convert_fusion.1 = bf16[2048,1792]{1,0:T(8,128)(2,1)} fusion(bf16[512,2048]{1,0:T(8,128)(2,1)S(1)} %copy-done.3, bf16[512,1792]{1,0:T(8,128)(2,1)S(1)} %copy-done.5), kind=kOutput, calls=%fused_computation.1 | convolution fusion | flops 3761766400 | bytes 11272192 | tf_op jit(solution)/shard_map/dot_general | solution.py:26
  161.2 0.0 copy-done.2
  161.2 0.0 copy-done.4
  161.2 0.0 copy-start.1
  161.2 0.0 copy-start
  161.2 6.1 %convolution_convert_fusion = bf16[1792,2048]{1,0:T(8,128)(2,1)} fusion(bf16[512,1792]{1,0:T(8,128)(2,1)S(1)} %copy-done.4, bf16[512,2048]{1,0:T(8,128)(2,1)S(1)} %copy-done.2), kind=kOutput, calls=%fused_computation | convolution fusion | flops 3761766400 | bytes 11272192 | tf_op jit(solution)/shard_map/dot_general | solution.py:26
  167.3 0.0 copy-done.1
  167.3 0.7 copy.12
  168.0 0.0 copy-done
  168.0 0.7 copy.13
Async XLA Ops:
  145.7 9.4 %copy-start.3 = (bf16[512,2048]{1,0:T(8,128)(2,1)S(1)}, bf16[512,2048]{1,0:T(8,128)(2,1)}, u32[]{:S(2)}) copy-start(bf16[512,2048]{1,0:T(8,128)(2,1)} %get-tuple-element.14) | copy-start | bytes 6291460
  145.7 9.4 %copy-start.5 = (bf16[512,1792]{1,0:T(8,128)(2,1)S(1)}, bf16[512,1792]{1,0:T(8,128)(2,1)}, u32[]{:S(2)}) copy-start(bf16[512,1792]{1,0:T(8,128)(2,1)} %get-tuple-element.16) | copy-start | bytes 5505028
  155.1 6.1 %copy-start.2 = (bf16[512,2048]{1,0:T(8,128)(2,1)S(1)}, bf16[512,2048]{1,0:T(8,128)(2,1)}, u32[]{:S(2)}) copy-start(bf16[512,2048]{1,0:T(8,128)(2,1)} %get-tuple-element.18) | copy-start | bytes 6291460
  155.1 6.1 %copy-start.4 = (bf16[512,1792]{1,0:T(8,128)(2,1)S(1)}, bf16[512,1792]{1,0:T(8,128)(2,1)}, u32[]{:S(2)}) copy-start(bf16[512,1792]{1,0:T(8,128)(2,1)} %get-tuple-element.17) | copy-start | bytes 5505028
  161.2 6.1 %copy-start.1 = (bf16[64,2048]{1,0:T(8,128)(2,1)S(1)}, bf16[64,2048]{1,0:T(8,128)(2,1)}, u32[]{:S(2)}) copy-start(bf16[64,2048]{1,0:T(8,128)(2,1)} %get-tuple-element.24) | copy-start | bytes 786436
  161.2 6.8 %copy-start = (bf16[64,2048]{1,0:T(8,128)(2,1)S(1)}, bf16[64,2048]{1,0:T(8,128)(2,1)}, u32[]{:S(2)}) copy-start(bf16[64,2048]{1,0:T(8,128)(2,1)} %get-tuple-element.25) | copy-start | bytes 786436

commit v2 on v1

--- a/solution.py
+++ b/solution.py
@@ -349,13 +349,26 @@
         save.wait()
 
 
+def step_of(z, i):
+    outer = (z == 0) | (z == 3)
+    swap = jnp.where(outer & (i == 2), 1, 0) - jnp.where(outer & (i == 3), 1, 0)
+    return i + swap
+
+
+LAST = ((0, 2), (1, 0), (2, 3), (3, 1))
+
+
+def last_source(z):
+    return jnp.where(z == 0, 1, jnp.where(z == 1, 3, jnp.where(z == 2, 0, 2)))
+
+
 def group_kernel(
     dims,
     x_ref, cot_ref, wg_hbm, wu_hbm, wd_hbm,
-    out_ref, tg_ref, x_out, cot_out, act_out, dg_out, du_out,
+    base_ref, last_ref, x_out, cot_out, act_out, dg_out, du_out,
     wg, wu, wd, x_full, cot_full, part, recv, h, acc, s_part, s_sib, s_sum, s_recv,
     w_sem, copy_sem, save_sem, x_ssem, x_rsem, c_ssem, c_rsem,
-    rs_ssem, rs_rsem, ag_ssem, ag_rsem, sib_ssem, sib_rsem, z_ssem, z_rsem,
+    rs_ssem, rs_rsem, ag_ssem, ag_rsem, sib_ssem, sib_rsem, z_ssem, z_rsem, last_sem,
 ):
     nz, tl, half, pw = dims
     feats = x_full.shape[1]
@@ -400,13 +413,13 @@
         )
 
     def index(u):
-        return lax.rem((u + 1) // 2, nz)
+        return u // 2
 
     def side(u):
-        return lax.rem(u + 1 + (index(u) == 0).astype(jnp.int32), 2)
+        return lax.rem(u, 2)
 
     def group(i):
-        return lax.rem(z + i * way + nz, nz)
+        return lax.rem(z + step_of(z, i) * way + nz, nz)
 
     def ends(u):
         flip = lax.rem(u, 2)
@@ -527,12 +540,7 @@
         g = group(i)
         span = block(g, tg)
         cols = block(side(u), hw)
-        opens = (u == 0) | ((i > 0) & (lax.rem(u, 2) == 1))
-
-        @pl.when((u > 0) & (u < nz))
-        def _():
-            x_stage(u)
-            c_stage(u)
+        opens = side(u) == 0
 
         @pl.when(opens)
         def _():
@@ -606,8 +614,6 @@
         i = index(u)
         g = group(i)
         span, hid = block(g, tg), block(side(u), hw)
-        slot = jnp.minimum(i, 1)
-        opens = (u == 0) | ((i > 0) & (lax.rem(u, 2) == 1))
         ag(u, 2, True).wait_recv()
         ag(u, 3, True).wait_recv()
         for save in saves(u):
@@ -618,22 +624,22 @@
             grad = dot_nt(h[1, span, hid], wg[cols, hid]) + dot_nt(h[2, span, hid], wu[cols, hid])
             return out, grad
 
-        @pl.when(opens)
+        @pl.when(side(u) == 0)
         def _():
             @pl.loop(0, feats // pw)
             def _(p):
                 cols = block(p, pw)
                 out, grad = products(cols)
-                acc[slot, 0, :, cols] = out
-                acc[slot, 1, :, cols] = grad
-
-        @pl.when(jnp.logical_not(opens))
+                acc[0, :, cols] = out
+                acc[1, :, cols] = grad
+
+        @pl.when(side(u) == 1)
         def _():
             @pl.loop(0, feats // pw)
             def _(p):
                 cols = block(p, pw)
                 for j, value in enumerate(products(cols)):
-                    value = (value + acc[slot, j, :, cols]).astype(BF16)
+                    value = (value + acc[j, :, cols]).astype(BF16)
                     for dd in range(2):
                         s_part[g, j, dd, :, cols] = value[dd * tl:(dd + 1) * tl]
 
@@ -644,7 +650,10 @@
         to_sibling(i).wait_recv()
         for j in range(2):
             s_sum[g, j] = (s_part[g, j, d].astype(F32) + s_sib[g, j].astype(F32)).astype(BF16)
-        to_col(i).start()
+
+        @pl.when((i > 0) & (i < nz - 1))
+        def _():
+            to_col(i).start()
 
     pl.semaphore_wait(barrier, 2 + nz - 1 + 1)
     x_first(x_ref)
@@ -677,22 +686,31 @@
         def _():
             relay(t)
 
-        @pl.when((t >= 5) & (t < units + 2) & (lax.rem(t, 2) == 1))
-        def _():
-            spread((t - 3) // 2)
-
-    to_sibling(0).wait_recv()
+        @pl.when((t > 0) & (t < nz))
+        def _():
+            x_stage(t)
+            c_stage(t)
+
+        @pl.when((t >= 4) & (lax.rem(t, 2) == 0))
+        def _():
+            spread(t // 2 - 2)
+
+    to_last = pltpu.make_async_copy(s_sum.at[group(nz - 1)], last_ref, last_sem)
+    to_last.start()
+    late = lax.rem(last_source(z) - z + nz, nz) - 1
 
     def landed(k):
         remote(s_sum.at[0], s_recv.at[k], z_ssem.at[0], z_rsem.at[k], sibling).wait_recv()
 
     for k in range(nz - 1):
-        landed(k)
-    for j, result in enumerate((out_ref, tg_ref)):
-        value = s_part[z, j, d].astype(F32) + s_sib[z, j].astype(F32)
-        for k in range(nz - 1):
-            value += s_recv[k, j].astype(F32)
-        result[...] = value.astype(BF16)
+        @pl.when(k != late)
+        def _():
+            landed(k)
+
+    value = s_sum[z].astype(F32)
+    for k in range(1, nz - 1):
+        value += s_recv[lax.rem(late + k, nz - 1)].astype(F32)
+    base_ref[...] = value
 
     x_drain()
     c_drain()
@@ -711,12 +729,13 @@
     def _(i):
         to_sibling(i).wait_send()
 
-        @pl.when(i > 0)
+        @pl.when((i > 0) & (i < nz - 1))
         def _():
             to_col(i).wait_send()
 
     x_save.wait()
     cot_save.wait()
+    to_last.wait()
 
 
 def per_device(n, nz, tokens, gate_weight, up_weight, down_weight, cotangent):
@@ -750,26 +769,27 @@
 
     vmem = pl.BlockSpec(memory_space=pltpu.VMEM)
     hbm = pl.BlockSpec(memory_space=pl.ANY)
-    if n == 4 and nz % 2 == 0 and tl % 32 == 0 and half % 256 == 0 and half >= 512:
-        output, tokens_grad, x_both, cot_both, act, dgate, dup = pl.pallas_call(
+    if n == 4 and nz == 4 and tl % 32 == 0 and half % 256 == 0 and half >= 512:
+        base, last, x_both, cot_both, act, dgate, dup = pl.pallas_call(
             functools.partial(group_kernel, (nz, tl, half, 2 * pw if parts % 2 == 0 else pw)),
             out_shape=(
-                sds(tl, feats), sds(tl, feats), sds(total, feats), sds(total, feats),
+                jax.ShapeDtypeStruct((2, tl, feats), F32), sds(2, tl, feats),
+                sds(total, feats), sds(total, feats),
                 sds(total, half), sds(total, half), sds(total, half),
             ),
             in_specs=[vmem, vmem, hbm, hbm, hbm],
-            out_specs=(vmem, vmem, hbm, hbm, hbm, hbm, hbm),
+            out_specs=(vmem, hbm, hbm, hbm, hbm, hbm, hbm),
             scratch_shapes=[
                 buf(feats, half), buf(feats, half), buf(half, feats),
                 buf(total, feats), buf(total, feats),
                 buf(nz, 3, 2 * tl, half), buf(nz, 3, 3, tl // 2, half),
-                buf(3, total, half), pltpu.VMEM((2, 2, 2 * tl, feats), F32),
+                buf(3, total, half), pltpu.VMEM((2, 2 * tl, feats), F32),
                 buf(nz, 2, 2, tl, feats), buf(nz, 2, tl, feats), buf(nz, 2, tl, feats),
                 buf(max(nz - 1, 1), 2, tl, feats),
                 sem(3, 2), sem(2), sem(2 * nz, 3),
                 sem(nz, 3), sem(nz * 2), sem(nz, 3), sem(nz * 2),
                 sem(2 * nz, 2, 3), sem(2 * nz, 2, 3), sem(2 * nz, 4), sem(2 * nz, 4),
-                sem(nz), sem(nz), sem(nz), sem(nz),
+                sem(nz), sem(nz), sem(nz), sem(nz), pltpu.SemaphoreType.DMA,
             ],
             compiler_params=pltpu.CompilerParams(
                 collective_id=1, has_side_effects=True, vmem_limit_bytes=60 * 2**20
@@ -779,6 +799,9 @@
                 transcendentals=0,
             ),
         )(tokens, cotangent, *weights)
+        sent = lax.ppermute(last, "col", LAST)
+        total_sums = (base + sent.astype(F32)).astype(BF16)
+        output, tokens_grad = total_sums[0], total_sums[1]
     else:
         sums = [
             buf(2, nz, tl, feats), buf(nz, tl, feats), buf(nz, tl, feats),

time: 169 us -> 152 us (0.90)
  Pallas kernels: 145 us -> 128 us
    pallas_call x1, Pallas kernels: 145 us -> 128 us  [per_device(): pl.pallas_call(functools.partial(group_kernel, (nz, tl, half, 2 * pw if p...]
  transfers between devices with their start and end apart: 0 -> 1, of which waited for: 0 -> 0; matrix products, arithmetic and copies ran while one was open for 0% -> 14% of each run, Pallas kernels for 0% -> 0%
where the time goes in v2:
time: 152 us; the launch traced here: 151 us
  Pallas kernels  128 us (84%)
  matrix products  21.6 us (14%)
    pallas_call x1, Pallas kernels, per_device(): pl.pallas_call(functools.partial(group_kernel, (nz, tl, half, 2 * pw if p...  128 us
    dot_general x3, matrix products, dot_tn(): lax.dot_general(left, right, (((0,), (0,)), ((), ())), preferred_element_...  21.6 us
  transfers between devices with their start and end apart: 1, of which 0 were waited for; matrix products, arithmetic and copies ran while one was open for 14% of the time, Pallas kernels for 0%

profile of v2, /device:TPU:0, one launch (start us, length us, event | category | flops | bytes accessed | tf_op | source)
XLA Modules:
  0.0 151.4 jit_solution(17243472172103881951)
XLA Ops:
  0.6 128.0 %shard_map.92 = (f32[2,64,2048]{2,1,0:T(8,128)}, bf16[2,64,2048]{2,1,0:T(8,128)(2,1)}, bf16[512,2048]{1,0:T(8,128)(2,1)}, bf16[512,2048]{1,0:T(8,128)(2,1)}, bf1...) custom-call(bf16[64,2048]{1,0:T(8,128)(2,1)} %x_ref.1, bf16[64,2048]{1,0:T(8,128)(2,1)} %cot_ref.1, ...), custom_call_target="tpu_custom_call" | custom-call | flops 22548578304 | bytes 29360128 | tf_op jit(solution)/shard_map/pallas_call | solution.py:773
  128.6 0.2 collective-permute-start
  128.9 0.0 copy-start.2
  128.9 0.0 copy-start.4
  128.9 9.4 %convolution_convert_fusion.2 = bf16[2048,1792]{1,0:T(8,128)(2,1)} fusion(bf16[512,2048]{1,0:T(8,128)(2,1)} %get-tuple-element.14, bf16[512,1792]{1,0:T(8,128)(2,1)} %get-tuple-element.15), kind=kOutput, calls=%fused_computation.2 | convolution fusion | flops 3761766400 | bytes 11272192 | tf_op jit(solution)/shard_map/dot_general | solution.py:26
  138.2 0.0 copy-done.2
  138.2 0.0 copy-done.4
  138.2 0.0 copy-start.1
  138.2 0.0 copy-start.3
  138.2 6.1 %convolution_convert_fusion.1 = bf16[2048,1792]{1,0:T(8,128)(2,1)} fusion(bf16[512,2048]{1,0:T(8,128)(2,1)S(1)} %copy-done.2, bf16[512,1792]{1,0:T(8,128)(2,1)S(1)} %copy-done.4), kind=kOutput, calls=%fused_computation.1 | convolution fusion | flops 3761766400 | bytes 11272192 | tf_op jit(solution)/shard_map/dot_general | solution.py:26
  144.4 0.0 copy-done.1
  144.4 0.0 copy-done.3
  144.4 0.0 copy-start
  144.4 6.1 %convolution_convert_fusion = bf16[1792,2048]{1,0:T(8,128)(2,1)} fusion(bf16[512,1792]{1,0:T(8,128)(2,1)S(1)} %copy-done.3, bf16[512,2048]{1,0:T(8,128)(2,1)S(1)} %copy-done.1), kind=kOutput, calls=%fused_computation | convolution fusion | flops 3761766400 | bytes 11272192 | tf_op jit(solution)/shard_map/dot_general | solution.py:26
  150.5 0.0 collective-permute-done
  150.5 0.0 copy-done
  150.5 0.1 add_convert_fusion
  150.6 0.8 slice_bitcast_fusion
Async XLA Ops:
  128.6 21.8 %collective-permute-start = (bf16[2,64,2048]{2,1,0:T(8,128)(2,1)}, bf16[2,64,2048]{2,1,0:T(8,128)(2,1)S(1)}, u32[]{:S(2)}, u32[]{:S(2)}) collective-permute-start(bf16[2,64,2048]{2,1,0:T(8,128)(2,1)} %get-tuple-element.13), channel_id=1, source_target_pairs={{0,4},{2,0},{4,6},{6,2},{1,5},{3,1},{5,7},{7,3},{8,12},{10,8},{12,... | collective-permute-start | bytes 1572872 | tf_op jit(solution)/shard_map/ppermute | solution.py:802
  128.9 9.4 %copy-start.2 = (bf16[512,2048]{1,0:T(8,128)(2,1)S(1)}, bf16[512,2048]{1,0:T(8,128)(2,1)}, u32[]{:S(2)}) copy-start(bf16[512,2048]{1,0:T(8,128)(2,1)} %get-tuple-element.14) | copy-start | bytes 6291460
  128.9 9.4 %copy-start.4 = (bf16[512,1792]{1,0:T(8,128)(2,1)S(1)}, bf16[512,1792]{1,0:T(8,128)(2,1)}, u32[]{:S(2)}) copy-start(bf16[512,1792]{1,0:T(8,128)(2,1)} %get-tuple-element.16) | copy-start | bytes 5505028
  138.2 6.1 %copy-start.1 = (bf16[512,2048]{1,0:T(8,128)(2,1)S(1)}, bf16[512,2048]{1,0:T(8,128)(2,1)}, u32[]{:S(2)}) copy-start(bf16[512,2048]{1,0:T(8,128)(2,1)} %get-tuple-element.18) | copy-start | bytes 6291460
  138.2 6.1 %copy-start.3 = (bf16[512,1792]{1,0:T(8,128)(2,1)S(1)}, bf16[512,1792]{1,0:T(8,128)(2,1)}, u32[]{:S(2)}) copy-start(bf16[512,1792]{1,0:T(8,128)(2,1)} %get-tuple-element.17) | copy-start | bytes 5505028
  144.4 6.1 %copy-start = (f32[2,64,2048]{2,1,0:T(8,128)S(1)}, f32[2,64,2048]{2,1,0:T(8,128)}, u32[]{:S(2)}) copy-start(f32[2,64,2048]{2,1,0:T(8,128)} %get-tuple-element.12) | copy-start | bytes 3145732

commit v3 on v2

--- a/solution.py
+++ b/solution.py
@@ -349,17 +349,8 @@
         save.wait()
 
 
-def step_of(z, i):
-    outer = (z == 0) | (z == 3)
-    swap = jnp.where(outer & (i == 2), 1, 0) - jnp.where(outer & (i == 3), 1, 0)
-    return i + swap
-
-
-LAST = ((0, 2), (1, 0), (2, 3), (3, 1))
-
-
-def last_source(z):
-    return jnp.where(z == 0, 1, jnp.where(z == 1, 3, jnp.where(z == 2, 0, 2)))
+VISITS = (0, 2, 3, 1)
+LAST = tuple((z, (z + VISITS[3]) % 4) for z in range(4))
 
 
 def group_kernel(
@@ -384,7 +375,6 @@
     ry = r + 2 - 4 * (r // 2)
     rd = 3 - r
     sibling = {"depth": 1 - d}
-    way = 1 - 2 * (z // max(nz // 2, 1))
 
     barrier = pltpu.get_barrier_semaphore()
     for where in (rx, ry):
@@ -394,7 +384,7 @@
     pl.semaphore_signal(barrier, inc=1, device_id=sibling, device_id_type=MESH)
 
     def load(i, s):
-        here = pl.ds(s * hw, hw)
+        here = block(s, hw)
         there = block(2 * d + s, hw)
         src, dst = (
             (wg_hbm.at[:, there], wg.at[:, here]),
@@ -419,7 +409,10 @@
         return lax.rem(u, 2)
 
     def group(i):
-        return lax.rem(z + step_of(z, i) * way + nz, nz)
+        if isinstance(i, int):
+            return lax.rem(z + VISITS[i], nz)
+        away = jnp.where(i == 0, 0, jnp.where(i == 3, 1, i + 1))
+        return lax.rem(z + away, nz)
 
     def ends(u):
         flip = lax.rem(u, 2)
@@ -497,11 +490,13 @@
     def rs(u, b, m):
         i = index(u)
         near, far = ends(u) if b == 0 else ends(u)[::-1]
-        owner = (rd, near, far)[m]
+        slot = m if m < 3 else m - 3
+        owner = (rd, near, far)[slot]
         to = far if m == 2 else near
         cols = span_of(u, b)
-        return remote(part.at[i, :, block(owner, tr), cols],
-                      recv.at[i, m, :, :, cols],
+        which = (pl.ds(0, 2), pl.ds(0, 2), pl.ds(0, 3), pl.ds(2, 1), pl.ds(2, 1))[m]
+        return remote(part.at[i, which, block(owner, tr), cols],
+                      recv.at[i, slot, which, :, cols],
                       rs_ssem.at[u, b, m], rs_rsem.at[u, b, m], {"row": to})
 
     def rows(g, owner):
@@ -535,43 +530,56 @@
     x_save = pltpu.make_async_copy(x_full, x_out, copy_sem.at[0])
     cot_save = pltpu.make_async_copy(cot_full, cot_out, copy_sem.at[1])
 
-    def compute(u):
+    def gate_up(u):
         i = index(u)
         g = group(i)
         span = block(g, tg)
         cols = block(side(u), hw)
-        opens = side(u) == 0
-
-        @pl.when(opens)
+
+        @pl.when((u == 2) | (u == 4))
+        def _():
+            x_stage(1 + u // 2)
+
+        @pl.when(side(u) == 0)
         def _():
             x_other(g)
 
-        @pl.when(u == 0)
-        def _():
-            load(0, 0).wait()
-            load(1, 0).wait()
-
-        @pl.when(u == 1)
-        def _():
-            for k in range(3):
-                load(k, 1).wait()
+        @pl.when(u < 2)
+        def _():
+            load(0, u).wait()
+            load(1, u).wait()
 
         part[i, 0, :, cols] = dot_nn(x_full[span, :], wg[:, cols]).astype(BF16)
         part[i, 1, :, cols] = dot_nn(x_full[span, :], wu[:, cols]).astype(BF16)
-
-        @pl.when(opens)
+        for m in range(2):
+            for b in range(2):
+                rs(u, b, m).start()
+
+    def hidden_grad(u):
+        i = index(u)
+        g = group(i)
+        span = block(g, tg)
+        cols = block(side(u), hw)
+
+        @pl.when((u == 2) | (u == 4))
+        def _():
+            c_stage(1 + u // 2)
+
+        @pl.when(side(u) == 0)
         def _():
             c_other(g)
 
+        @pl.when(u < 2)
+        def _():
+            load(2, u).wait()
+
         @pl.when(u == 0)
         def _():
-            load(2, 0).wait()
             for k in range(3):
                 load(k, 1).start()
 
         part[i, 2, :, cols] = dot_nt(cot_full[span, :], wd[cols, :]).astype(BF16)
-
-        for m in range(2):
+        for m in range(3, 5):
             for b in range(2):
                 rs(u, b, m).start()
 
@@ -579,6 +587,7 @@
         i = index(u)
         for b in range(2):
             rs(u, b, 0).wait_recv()
+            rs(u, b, 3).wait_recv()
             spot, cols = block(ends(u)[1 - b], tr), span_of(u, b)
             part[i, :, spot, cols] = (
                 part[i, :, spot, cols].astype(F32) + recv[i, 0, :, :, cols].astype(F32)
@@ -589,8 +598,8 @@
         i = index(u)
         own = rows(group(i), r)
         for b in range(2):
-            rs(u, b, 1).wait_recv()
-            rs(u, b, 2).wait_recv()
+            for m in (1, 4, 2):
+                rs(u, b, m).wait_recv()
             cols = span_of(u, b)
             gate, up, dact = (
                 part[i, j, block(r, tr), cols].astype(F32)
@@ -663,53 +672,57 @@
     def _(t):
         @pl.when(t < units)
         def _():
-            compute(t)
+            gate_up(t)
+
+        @pl.when((t >= 2) & (t < units + 2))
+        def _():
+            forward(t - 2)
+
+        @pl.when(t < units)
+        def _():
+            hidden_grad(t)
+
+        @pl.when((t >= 1) & (t < units + 1))
+        def _():
+            hidden(t - 1)
+
+        @pl.when(t >= 3)
+        def _():
+            project(t - 3)
+
+        @pl.when(t == 1)
+        def _():
+            c_stage(1)
+
+        @pl.when(t < units)
+        def _():
+            relay(t)
+
+        @pl.when(t == 0)
+        def _():
+            x_stage(1)
 
         @pl.when(t == units - 2)
         def _():
             x_save.start()
             cot_save.start()
 
-        @pl.when((t >= 2) & (t < units + 2))
-        def _():
-            forward(t - 2)
-
-        @pl.when((t >= 1) & (t < units + 1))
-        def _():
-            hidden(t - 1)
-
-        @pl.when(t >= 3)
-        def _():
-            project(t - 3)
-
-        @pl.when(t < units)
-        def _():
-            relay(t)
-
-        @pl.when((t > 0) & (t < nz))
-        def _():
-            x_stage(t)
-            c_stage(t)
-
         @pl.when((t >= 4) & (lax.rem(t, 2) == 0))
         def _():
             spread(t // 2 - 2)
 
     to_last = pltpu.make_async_copy(s_sum.at[group(nz - 1)], last_ref, last_sem)
     to_last.start()
-    late = lax.rem(last_source(z) - z + nz, nz) - 1
 
     def landed(k):
         remote(s_sum.at[0], s_recv.at[k], z_ssem.at[0], z_rsem.at[k], sibling).wait_recv()
 
-    for k in range(nz - 1):
-        @pl.when(k != late)
-        def _():
-            landed(k)
+    for k in range(nz - 2):
+        landed(k)
 
     value = s_sum[z].astype(F32)
-    for k in range(1, nz - 1):
-        value += s_recv[lax.rem(late + k, nz - 1)].astype(F32)
+    for k in range(nz - 2):
+        value += s_recv[k].astype(F32)
     base_ref[...] = value
 
     x_drain()
@@ -718,7 +731,7 @@
     @pl.loop(0, units)
     def _(u):
         for b in range(2):
-            for m in range(3):
+            for m in range(5):
                 rs(u, b, m).wait_send()
         for m in range(4):
             ag(u, m).wait_send()
@@ -785,10 +798,10 @@
                 buf(nz, 3, 2 * tl, half), buf(nz, 3, 3, tl // 2, half),
                 buf(3, total, half), pltpu.VMEM((2, 2 * tl, feats), F32),
                 buf(nz, 2, 2, tl, feats), buf(nz, 2, tl, feats), buf(nz, 2, tl, feats),
-                buf(max(nz - 1, 1), 2, tl, feats),
+                buf(nz - 2, 2, tl, feats),
                 sem(3, 2), sem(2), sem(2 * nz, 3),
                 sem(nz, 3), sem(nz * 2), sem(nz, 3), sem(nz * 2),
-                sem(2 * nz, 2, 3), sem(2 * nz, 2, 3), sem(2 * nz, 4), sem(2 * nz, 4),
+                sem(2 * nz, 2, 5), sem(2 * nz, 2, 5), sem(2 * nz, 4), sem(2 * nz, 4),
                 sem(nz), sem(nz), sem(nz), sem(nz), pltpu.SemaphoreType.DMA,
             ],
             compiler_params=pltpu.CompilerParams(

time: 152 us -> 144 us (0.947)
  Pallas kernels: 128 us -> 120 us
    pallas_call x1, Pallas kernels: 128 us -> 120 us  [per_device(): pl.pallas_call(functools.partial(group_kernel, (nz, tl, half, 2 * pw if p...]
  transfers between devices with their start and end apart: 1 -> 1, of which waited for: 0 -> 0; matrix products, arithmetic and copies ran while one was open for 14% -> 15% of each run, Pallas kernels for 0% -> 0%
where the time goes in v3:
time: 144 us
  Pallas kernels  120 us (83%)
  matrix products  21.5 us (15%)
    pallas_call x1, Pallas kernels, per_device(): pl.pallas_call(functools.partial(group_kernel, (nz, tl, half, 2 * pw if p...  120 us
    dot_general x3, matrix products, dot_tn(): lax.dot_general(left, right, (((0,), (0,)), ((), ())), preferred_element_...  21.5 us
  transfers between devices with their start and end apart: 1, of which 0 were waited for; matrix products, arithmetic and copies ran while one was open for 15% of the time, Pallas kernels for 0%

profile of v3, /device:TPU:0, one launch (start us, length us, event | category | flops | bytes accessed | tf_op | source)
XLA Modules:
  0.0 144.1 jit_solution(14031627265976456840)
XLA Ops:
  0.6 120.1 %shard_map.92 = (f32[2,64,2048]{2,1,0:T(8,128)}, bf16[2,64,2048]{2,1,0:T(8,128)(2,1)}, bf16[512,2048]{1,0:T(8,128)(2,1)}, bf16[512,2048]{1,0:T(8,128)(2,1)}, bf1...) custom-call(bf16[64,2048]{1,0:T(8,128)(2,1)} %x_ref.1, bf16[64,2048]{1,0:T(8,128)(2,1)} %cot_ref.1, ...), custom_call_target="tpu_custom_call" | custom-call | flops 22548578304 | bytes 29360128 | tf_op jit(solution)/shard_map/pallas_call | solution.py:786
  120.7 0.8 collective-permute-start
  121.6 0.0 copy-start.2
  121.6 0.0 copy-start.4
  121.6 9.4 %convolution_convert_fusion.2 = bf16[2048,1792]{1,0:T(8,128)(2,1)} fusion(bf16[512,2048]{1,0:T(8,128)(2,1)} %get-tuple-element.14, bf16[512,1792]{1,0:T(8,128)(2,1)} %get-tuple-element.15), kind=kOutput, calls=%fused_computation.2 | convolution fusion | flops 3761766400 | bytes 11272192 | tf_op jit(solution)/shard_map/dot_general | solution.py:26
  130.9 0.0 copy-done.2
  130.9 0.0 copy-done.4
  130.9 0.0 copy-start.1
  131.0 0.0 copy-start.3
  131.0 6.1 %convolution_convert_fusion.1 = bf16[2048,1792]{1,0:T(8,128)(2,1)} fusion(bf16[512,2048]{1,0:T(8,128)(2,1)S(1)} %copy-done.2, bf16[512,1792]{1,0:T(8,128)(2,1)S(1)} %copy-done.4), kind=kOutput, calls=%fused_computation.1 | convolution fusion | flops 3761766400 | bytes 11272192 | tf_op jit(solution)/shard_map/dot_general | solution.py:26
  137.1 0.0 copy-done.1
  137.1 0.0 copy-done.3
  137.1 0.0 copy-start
  137.1 6.1 %convolution_convert_fusion = bf16[1792,2048]{1,0:T(8,128)(2,1)} fusion(bf16[512,1792]{1,0:T(8,128)(2,1)S(1)} %copy-done.3, bf16[512,2048]{1,0:T(8,128)(2,1)S(1)} %copy-done.1), kind=kOutput, calls=%fused_computation | convolution fusion | flops 3761766400 | bytes 11272192 | tf_op jit(solution)/shard_map/dot_general | solution.py:26
  143.2 0.0 collective-permute-done
  143.2 0.0 copy-done
  143.2 0.1 add_convert_fusion
  143.3 0.8 slice_bitcast_fusion
Async XLA Ops:
  120.7 22.4 %collective-permute-start = (bf16[2,64,2048]{2,1,0:T(8,128)(2,1)}, bf16[2,64,2048]{2,1,0:T(8,128)(2,1)S(1)}, u32[]{:S(2)}, u32[]{:S(2)}) collective-permute-start(bf16[2,64,2048]{2,1,0:T(8,128)(2,1)} %get-tuple-element.13), channel_id=1, source_target_pairs={{0,2},{2,4},{4,6},{6,0},{1,3},{3,5},{5,7},{7,1},{8,10},{10,12},{12... | collective-permute-start | bytes 1572872 | tf_op jit(solution)/shard_map/ppermute | solution.py:815
  121.6 9.4 %copy-start.2 = (bf16[512,2048]{1,0:T(8,128)(2,1)S(1)}, bf16[512,2048]{1,0:T(8,128)(2,1)}, u32[]{:S(2)}) copy-start(bf16[512,2048]{1,0:T(8,128)(2,1)} %get-tuple-element.14) | copy-start | bytes 6291460
  121.6 9.4 %copy-start.4 = (bf16[512,1792]{1,0:T(8,128)(2,1)S(1)}, bf16[512,1792]{1,0:T(8,128)(2,1)}, u32[]{:S(2)}) copy-start(bf16[512,1792]{1,0:T(8,128)(2,1)} %get-tuple-element.16) | copy-start | bytes 5505028
  130.9 6.1 %copy-start.1 = (bf16[512,2048]{1,0:T(8,128)(2,1)S(1)}, bf16[512,2048]{1,0:T(8,128)(2,1)}, u32[]{:S(2)}) copy-start(bf16[512,2048]{1,0:T(8,128)(2,1)} %get-tuple-element.18) | copy-start | bytes 6291460
  131.0 6.1 %copy-start.3 = (bf16[512,1792]{1,0:T(8,128)(2,1)S(1)}, bf16[512,1792]{1,0:T(8,128)(2,1)}, u32[]{:S(2)}) copy-start(bf16[512,1792]{1,0:T(8,128)(2,1)} %get-tuple-element.17) | copy-start | bytes 5505028
  137.1 6.1 %copy-start = (f32[2,64,2048]{2,1,0:T(8,128)S(1)}, f32[2,64,2048]{2,1,0:T(8,128)}, u32[]{:S(2)}) copy-start(f32[2,64,2048]{2,1,0:T(8,128)} %get-tuple-element.12) | copy-start | bytes 3145732

commit v4 on v3

--- a/solution.py
+++ b/solution.py
@@ -356,7 +356,7 @@
 def group_kernel(
     dims,
     x_ref, cot_ref, wg_hbm, wu_hbm, wd_hbm,
-    base_ref, last_ref, x_out, cot_out, act_out, dg_out, du_out,
+    out_ref, tg_ref, last_ref, x_out, cot_out, act_out, dg_out, du_out,
     wg, wu, wd, x_full, cot_full, part, recv, h, acc, s_part, s_sib, s_sum, s_recv,
     w_sem, copy_sem, save_sem, x_ssem, x_rsem, c_ssem, c_rsem,
     rs_ssem, rs_rsem, ag_ssem, ag_rsem, sib_ssem, sib_rsem, z_ssem, z_rsem, last_sem,
@@ -674,6 +674,10 @@
         def _():
             gate_up(t)
 
+        @pl.when(t >= 3)
+        def _():
+            project(t - 3)
+
         @pl.when((t >= 2) & (t < units + 2))
         def _():
             forward(t - 2)
@@ -686,9 +690,9 @@
         def _():
             hidden(t - 1)
 
-        @pl.when(t >= 3)
-        def _():
-            project(t - 3)
+        @pl.when((t >= 4) & (lax.rem(t, 2) == 0))
+        def _():
+            spread((t - 4) // 2)
 
         @pl.when(t == 1)
         def _():
@@ -707,10 +711,6 @@
             x_save.start()
             cot_save.start()
 
-        @pl.when((t >= 4) & (lax.rem(t, 2) == 0))
-        def _():
-            spread(t // 2 - 2)
-
     to_last = pltpu.make_async_copy(s_sum.at[group(nz - 1)], last_ref, last_sem)
     to_last.start()
 
@@ -720,10 +720,11 @@
     for k in range(nz - 2):
         landed(k)
 
-    value = s_sum[z].astype(F32)
-    for k in range(nz - 2):
-        value += s_recv[k].astype(F32)
-    base_ref[...] = value
+    for j, result in enumerate((out_ref, tg_ref)):
+        value = s_sum[z, j].astype(F32)
+        for k in range(nz - 2):
+            value += s_recv[k, j].astype(F32)
+        result[...] = value
 
     x_drain()
     c_drain()
@@ -749,6 +750,83 @@
     x_save.wait()
     cot_save.wait()
     to_last.wait()
+
+
+def weight_kernel(
+    x_hbm, dg_hbm, du_hbm, act_hbm, cot_hbm, gate_hbm, up_hbm, down_hbm,
+    x, dg, du, act, cot, gate_tile, up_tile, down_tile, in_sem, out_sem,
+):
+    loads = [
+        pltpu.make_async_copy(src, dst, in_sem.at[k])
+        for k, (src, dst) in enumerate(
+            ((x_hbm, x), (dg_hbm, dg), (du_hbm, du), (act_hbm, act), (cot_hbm, cot)))
+    ]
+    for load in loads:
+        load.start()
+
+    def product(k, left, right, tile, result):
+        size, width = tile.shape[1], right.shape[1] // 2
+        tiles = left.shape[1] // size
+
+        def save(i):
+            slot = lax.rem(i, 2)
+            return pltpu.make_async_copy(tile.at[slot], result.at[block(i, size)], out_sem.at[k, slot])
+
+        @pl.loop(0, tiles)
+        def _(i):
+            @pl.when(i > 1)
+            def _():
+                save(i - 2).wait()
+
+            rows, slot = left[:, block(i, size)], lax.rem(i, 2)
+            for cols in (pl.ds(0, width), pl.ds(width, width)):
+                tile[slot, :, cols] = dot_tn(rows, right[:, cols]).astype(BF16)
+            save(i).start()
+
+        return [save(i) for i in range(max(tiles - 2, 0), tiles)]
+
+    loads[0].wait()
+    loads[1].wait()
+    left_over = product(0, x, dg, gate_tile, gate_hbm)
+    loads[2].wait()
+    left_over += product(1, x, du, up_tile, up_hbm)
+    loads[3].wait()
+    loads[4].wait()
+    left_over += product(2, act, cot, down_tile, down_hbm)
+    for save in left_over:
+        save.wait()
+
+
+def weight_grads(x, dgate, dup, act, cot):
+    total, feats = x.shape
+    half = act.shape[1]
+    tall, short = feats // 2, half // 2
+    hbm = pl.BlockSpec(memory_space=pl.ANY)
+
+    def buf(*shape):
+        return pltpu.VMEM(shape, BF16)
+
+    return pl.pallas_call(
+        weight_kernel,
+        in_specs=[hbm] * 5,
+        out_specs=(hbm, hbm, hbm),
+        out_shape=(
+            jax.ShapeDtypeStruct((feats, half), BF16),
+            jax.ShapeDtypeStruct((feats, half), BF16),
+            jax.ShapeDtypeStruct((half, feats), BF16),
+        ),
+        scratch_shapes=[
+            buf(total, feats), buf(total, half), buf(total, half), buf(total, half), buf(total, feats),
+            buf(2, tall, half), buf(2, tall, half), buf(2, short, feats),
+            pltpu.SemaphoreType.DMA((5,)), pltpu.SemaphoreType.DMA((3, 2)),
+        ],
+        compiler_params=pltpu.CompilerParams(vmem_limit_bytes=60 * 2**20),
+        cost_estimate=pl.CostEstimate(
+            flops=6 * total * feats * half,
+            bytes_accessed=6 * feats * half + 4 * total * feats + 6 * total * half,
+            transcendentals=0,
+        ),
+    )(x, dgate, dup, act, cot)
 
 
 def per_device(n, nz, tokens, gate_weight, up_weight, down_weight, cotangent):
@@ -783,15 +861,16 @@
     vmem = pl.BlockSpec(memory_space=pltpu.VMEM)
     hbm = pl.BlockSpec(memory_space=pl.ANY)
     if n == 4 and nz == 4 and tl % 32 == 0 and half % 256 == 0 and half >= 512:
-        base, last, x_both, cot_both, act, dgate, dup = pl.pallas_call(
+        out_part, tg_part, last, x_both, cot_both, act, dgate, dup = pl.pallas_call(
             functools.partial(group_kernel, (nz, tl, half, 2 * pw if parts % 2 == 0 else pw)),
             out_shape=(
-                jax.ShapeDtypeStruct((2, tl, feats), F32), sds(2, tl, feats),
+                jax.ShapeDtypeStruct((tl, feats), F32), jax.ShapeDtypeStruct((tl, feats), F32),
+                sds(2, tl, feats),
                 sds(total, feats), sds(total, feats),
                 sds(total, half), sds(total, half), sds(total, half),
             ),
             in_specs=[vmem, vmem, hbm, hbm, hbm],
-            out_specs=(vmem, hbm, hbm, hbm, hbm, hbm, hbm),
+            out_specs=(vmem, vmem, hbm, hbm, hbm, hbm, hbm, hbm),
             scratch_shapes=[
                 buf(feats, half), buf(feats, half), buf(half, feats),
                 buf(total, feats), buf(total, feats),
@@ -813,8 +892,10 @@
             ),
         )(tokens, cotangent, *weights)
         sent = lax.ppermute(last, "col", LAST)
-        total_sums = (base + sent.astype(F32)).astype(BF16)
-        output, tokens_grad = total_sums[0], total_sums[1]
+        output = (out_part + sent[0].astype(F32)).astype(BF16)
+        tokens_grad = (tg_part + sent[1].astype(F32)).astype(BF16)
+        if feats % 256 == 0:
+            return (output, tokens_grad, *weight_grads(x_both, dgate, dup, act, cot_both))
     else:
         sums = [
             buf(2, nz, tl, feats), buf(nz, tl, feats), buf(nz, tl, feats),

time: 144 us -> 137 us (0.951)
  matrix products: 21.5 us -> 0 us
  Pallas kernels: 120 us -> 135 us
    dot_general x3 -> x0, matrix products: 21.5 us -> none  [dot_tn(): lax.dot_general(left, right, (((0,), (0,)), ((), ())), preferred_element_...]
    pallas_call x0 -> x1, Pallas kernels: none -> 17.9 us  [weight_grads(): pl.pallas_call(weight_kernel, in_specs=[hbm] * 5, out_specs=(hbm, hbm, hb...]
    pallas_call x1, Pallas kernels: 120 us -> 117 us  [per_device(): pl.pallas_call(functools.partial(group_kernel, (nz, tl, half, 2 * pw if p...]
  transfers between devices with their start and end apart: 1 -> 1, of which waited for: 0 -> 0; matrix products, arithmetic and copies ran while one was open for 15% -> 0% of each run, Pallas kernels for 0% -> 13%
where the time goes in v4:
time: 137 us
  Pallas kernels  135 us (99%)
    pallas_call x1, Pallas kernels, per_device(): pl.pallas_call(functools.partial(group_kernel, (nz, tl, half, 2 * pw if p...  117 us
    pallas_call x1, Pallas kernels, weight_grads(): pl.pallas_call(weight_kernel, in_specs=[hbm] * 5, out_specs=(hbm, hbm, hb...  17.9 us
  transfers between devices with their start and end apart: 1, of which 0 were waited for; matrix products, arithmetic and copies ran while one was open for 0% of the time, Pallas kernels for 13%

profile of v4, /device:TPU:0, one launch (start us, length us, event | category | flops | bytes accessed | tf_op | source)
XLA Modules:
  0.0 136.8 jit_solution(8733795445522474214)
XLA Ops:
  0.6 117.3 %shard_map.92 = (f32[64,2048]{1,0:T(8,128)}, f32[64,2048]{1,0:T(8,128)}, bf16[2,64,2048]{2,1,0:T(8,128)(2,1)}, bf16[512,2048]{1,0:T(8,128)(2,1)}, bf16[512,2048]...) custom-call(bf16[64,2048]{1,0:T(8,128)(2,1)} %x_ref.1, ...), custom_call_target="tpu_custom_call" | custom-call | flops 22548578304 | bytes 29360128 | tf_op jit(solution)/shard_map/pallas_call | solution.py:864
  117.9 0.1 collective-permute-start
  118.0 0.0 copy-start
  118.0 0.0 copy-start.1
  118.0 17.9 %shard_map.93 = (bf16[2048,1792]{1,0:T(8,128)(2,1)}, bf16[2048,1792]{1,0:T(8,128)(2,1)}, bf16[1792,2048]{1,0:T(8,128)(2,1)}) custom-call(bf16[512,2048]{1,0:T(8,128)(2,1)} %get-tuple-element.19.x_hbm, bf16[512,1792]{1,0:T(8,128)(2,1)} %get-tuple-element.20.dg_hbm, bf16[512,1792]{1,0:T(8,128)(2,1)} %get-tuple-element.21.du_hbm, ...), custom_call_target="tpu_custom_call" | custom-call | flops 11274289152 | bytes 31719424 | tf_op jit(solution)/shard_map/pallas_call | solution.py:809
  135.9 0.0 collective-permute-done
  135.9 0.0 copy-done
  135.9 0.0 copy-done.1
  135.9 0.9 fusion
Async XLA Ops:
  117.9 18.0 %collective-permute-start = (bf16[2,64,2048]{2,1,0:T(8,128)(2,1)}, bf16[2,64,2048]{2,1,0:T(8,128)(2,1)S(1)}, u32[]{:S(2)}, u32[]{:S(2)}) collective-permute-start(bf16[2,64,2048]{2,1,0:T(8,128)(2,1)} %get-tuple-element.17), channel_id=1, source_target_pairs={{0,2},{2,4},{4,6},{6,0},{1,3},{3,5},{5,7},{7,1},{8,10},{10,12},{12... | collective-permute-start | bytes 1572872 | tf_op jit(solution)/shard_map/ppermute | solution.py:894
  118.0 17.9 %copy-start = (f32[64,2048]{1,0:T(8,128)S(1)}, f32[64,2048]{1,0:T(8,128)}, u32[]{:S(2)}) copy-start(f32[64,2048]{1,0:T(8,128)} %get-tuple-element.16) | copy-start | bytes 1572868
  118.0 17.9 %copy-start.1 = (f32[64,2048]{1,0:T(8,128)S(1)}, f32[64,2048]{1,0:T(8,128)}, u32[]{:S(2)}) copy-start(f32[64,2048]{1,0:T(8,128)} %get-tuple-element.18) | copy-start | bytes 1572868

commit v5 on v4

--- a/solution.py
+++ b/solution.py
@@ -356,10 +356,10 @@
 def group_kernel(
     dims,
     x_ref, cot_ref, wg_hbm, wu_hbm, wd_hbm,
-    out_ref, tg_ref, last_ref, x_out, cot_out, act_out, dg_out, du_out,
-    wg, wu, wd, x_full, cot_full, part, recv, h, acc, s_part, s_sib, s_sum, s_recv,
+    out_hbm, tg_hbm, last_ref, x_out, cot_out, act_out, dg_out, du_out,
+    wg, wu, wd, x_full, cot_full, part, recv, h, acc, s_part, s_sib, s_sum, s_recv, base,
     w_sem, copy_sem, save_sem, x_ssem, x_rsem, c_ssem, c_rsem,
-    rs_ssem, rs_rsem, ag_ssem, ag_rsem, sib_ssem, sib_rsem, z_ssem, z_rsem, last_sem,
+    rs_ssem, rs_rsem, ag_ssem, ag_rsem, sib_ssem, sib_rsem, z_ssem, z_rsem, last_sem, base_sem,
 ):
     nz, tl, half, pw = dims
     feats = x_full.shape[1]
@@ -660,77 +660,12 @@
         for j in range(2):
             s_sum[g, j] = (s_part[g, j, d].astype(F32) + s_sib[g, j].astype(F32)).astype(BF16)
 
+
         @pl.when((i > 0) & (i < nz - 1))
         def _():
             to_col(i).start()
 
-    pl.semaphore_wait(barrier, 2 + nz - 1 + 1)
-    x_first(x_ref)
-    c_first(cot_ref)
-
-    @pl.loop(0, units + 3)
-    def _(t):
-        @pl.when(t < units)
-        def _():
-            gate_up(t)
-
-        @pl.when(t >= 3)
-        def _():
-            project(t - 3)
-
-        @pl.when((t >= 2) & (t < units + 2))
-        def _():
-            forward(t - 2)
-
-        @pl.when(t < units)
-        def _():
-            hidden_grad(t)
-
-        @pl.when((t >= 1) & (t < units + 1))
-        def _():
-            hidden(t - 1)
-
-        @pl.when((t >= 4) & (lax.rem(t, 2) == 0))
-        def _():
-            spread((t - 4) // 2)
-
-        @pl.when(t == 1)
-        def _():
-            c_stage(1)
-
-        @pl.when(t < units)
-        def _():
-            relay(t)
-
-        @pl.when(t == 0)
-        def _():
-            x_stage(1)
-
-        @pl.when(t == units - 2)
-        def _():
-            x_save.start()
-            cot_save.start()
-
-    to_last = pltpu.make_async_copy(s_sum.at[group(nz - 1)], last_ref, last_sem)
-    to_last.start()
-
-    def landed(k):
-        remote(s_sum.at[0], s_recv.at[k], z_ssem.at[0], z_rsem.at[k], sibling).wait_recv()
-
-    for k in range(nz - 2):
-        landed(k)
-
-    for j, result in enumerate((out_ref, tg_ref)):
-        value = s_sum[z, j].astype(F32)
-        for k in range(nz - 2):
-            value += s_recv[k, j].astype(F32)
-        result[...] = value
-
-    x_drain()
-    c_drain()
-
-    @pl.loop(0, units)
-    def _(u):
+    def settle(u):
         for b in range(2):
             for m in range(5):
                 rs(u, b, m).wait_send()
@@ -739,16 +674,92 @@
         for save in saves(u):
             save.wait()
 
-    @pl.loop(0, nz)
-    def _(i):
+    pl.semaphore_wait(barrier, 2 + nz - 1 + 1)
+    x_first(x_ref)
+    c_first(cot_ref)
+
+    @pl.loop(0, units + 3)
+    def _(t):
+        @pl.when(t < units)
+        def _():
+            gate_up(t)
+
+        @pl.when(t >= 3)
+        def _():
+            project(t - 3)
+
+        @pl.when((t >= 2) & (t < units + 2))
+        def _():
+            forward(t - 2)
+
+        @pl.when(t < units)
+        def _():
+            hidden_grad(t)
+
+        @pl.when((t >= 1) & (t < units + 1))
+        def _():
+            hidden(t - 1)
+
+        @pl.when((t >= 4) & (t < units + 2) & (lax.rem(t, 2) == 0))
+        def _():
+            spread((t - 4) // 2)
+
+        @pl.when(t == 1)
+        def _():
+            c_stage(1)
+
+        @pl.when(t < units)
+        def _():
+            relay(t)
+
+        @pl.when(t == 0)
+        def _():
+            x_stage(1)
+
+        @pl.when(t >= 5)
+        def _():
+            settle(t - 5)
+
+        @pl.when(t == units)
+        def _():
+            x_drain()
+            c_drain()
+
+        @pl.when(t == units - 2)
+        def _():
+            x_save.start()
+            cot_save.start()
+
+    def landed(k):
+        remote(s_sum.at[0], s_recv.at[k], z_ssem.at[0], z_rsem.at[k], sibling).wait_recv()
+
+    for k in range(nz - 2):
+        landed(k)
+
+    to_base = [
+        pltpu.make_async_copy(base.at[j], result, base_sem.at[j])
+        for j, result in enumerate((out_hbm, tg_hbm))
+    ]
+    for j in range(2):
+        value = s_sum[z, j].astype(F32)
+        for k in range(nz - 2):
+            value += s_recv[k, j].astype(F32)
+        base[j] = value
+        to_base[j].start()
+
+    settle(units - 2)
+    settle(units - 1)
+    for i in range(1, nz - 1):
+        to_col(i).wait_send()
+    spread(nz - 1)
+    to_last = pltpu.make_async_copy(s_sum.at[group(nz - 1)], last_ref, last_sem)
+    to_last.start()
+    for i in range(nz):
         to_sibling(i).wait_send()
-
-        @pl.when((i > 0) & (i < nz - 1))
-        def _():
-            to_col(i).wait_send()
-
     x_save.wait()
     cot_save.wait()
+    for copy in to_base:
+        copy.wait()
     to_last.wait()
 
 
@@ -756,44 +767,47 @@
     x_hbm, dg_hbm, du_hbm, act_hbm, cot_hbm, gate_hbm, up_hbm, down_hbm,
     x, dg, du, act, cot, gate_tile, up_tile, down_tile, in_sem, out_sem,
 ):
-    loads = [
-        pltpu.make_async_copy(src, dst, in_sem.at[k])
-        for k, (src, dst) in enumerate(
-            ((x_hbm, x), (dg_hbm, dg), (du_hbm, du), (act_hbm, act), (cot_hbm, cot)))
-    ]
-    for load in loads:
-        load.start()
-
-    def product(k, left, right, tile, result):
-        size, width = tile.shape[1], right.shape[1] // 2
-        tiles = left.shape[1] // size
-
-        def save(i):
-            slot = lax.rem(i, 2)
-            return pltpu.make_async_copy(tile.at[slot], result.at[block(i, size)], out_sem.at[k, slot])
-
-        @pl.loop(0, tiles)
-        def _(i):
-            @pl.when(i > 1)
-            def _():
-                save(i - 2).wait()
-
-            rows, slot = left[:, block(i, size)], lax.rem(i, 2)
-            for cols in (pl.ds(0, width), pl.ds(width, width)):
-                tile[slot, :, cols] = dot_tn(rows, right[:, cols]).astype(BF16)
-            save(i).start()
-
-        return [save(i) for i in range(max(tiles - 2, 0), tiles)]
-
-    loads[0].wait()
-    loads[1].wait()
-    left_over = product(0, x, dg, gate_tile, gate_hbm)
-    loads[2].wait()
-    left_over += product(1, x, du, up_tile, up_hbm)
-    loads[3].wait()
-    loads[4].wait()
-    left_over += product(2, act, cot, down_tile, down_hbm)
-    for save in left_over:
+    halves = []
+    for k, (src, dst) in enumerate(((x_hbm, x), (dg_hbm, dg), (du_hbm, du), (act_hbm, act), (cot_hbm, cot))):
+        width = src.shape[1] // 2
+        halves.append([
+            pltpu.make_async_copy(src.at[:, cols], dst.at[:, cols], in_sem.at[k, c])
+            for c, cols in enumerate((pl.ds(0, width), pl.ds(width, width)))
+        ])
+
+    def product(k, left, right, tile, result, before):
+        rows, width = left.shape[1] // 2, right.shape[1] // 2
+        saves = []
+        for i in range(2):
+            for c in range(2):
+                for step in before.pop((i, c), ()):
+                    step()
+                here, cols = pl.ds(i * rows, rows), pl.ds(c * width, width)
+                tile[i, :, cols] = dot_tn(left[:, here], right[:, cols]).astype(BF16)
+                save = pltpu.make_async_copy(
+                    tile.at[i, :, cols], result.at[here, cols], out_sem.at[k, i, c])
+                save.start()
+                saves.append(save)
+        return saves
+
+    def start(*names):
+        return [halves[k][c].start for k, c in names]
+
+    def wait(*names):
+        return [halves[k][c].wait for k, c in names]
+
+    for step in start((0, 0), (1, 0), (1, 1), (0, 1)):
+        step()
+    saves = product(0, x, dg, gate_tile, gate_hbm, {
+        (0, 0): wait((0, 0), (1, 0)) + start((2, 0), (2, 1)),
+        (0, 1): wait((1, 1)),
+        (1, 0): wait((0, 1)) + start((3, 0), (4, 0), (4, 1), (3, 1)),
+    })
+    saves += product(1, x, du, up_tile, up_hbm, {(0, 0): wait((2, 0)), (0, 1): wait((2, 1))})
+    saves += product(2, act, cot, down_tile, down_hbm, {
+        (0, 0): wait((3, 0), (4, 0)), (0, 1): wait((4, 1)), (1, 0): wait((3, 1)),
+    })
+    for save in saves:
         save.wait()
 
 
@@ -818,7 +832,7 @@
         scratch_shapes=[
             buf(total, feats), buf(total, half), buf(total, half), buf(total, half), buf(total, feats),
             buf(2, tall, half), buf(2, tall, half), buf(2, short, feats),
-            pltpu.SemaphoreType.DMA((5,)), pltpu.SemaphoreType.DMA((3, 2)),
+            pltpu.SemaphoreType.DMA((5, 2)), pltpu.SemaphoreType.DMA((3, 2, 2)),
         ],
         compiler_params=pltpu.CompilerParams(vmem_limit_bytes=60 * 2**20),
         cost_estimate=pl.CostEstimate(
@@ -870,18 +884,18 @@
                 sds(total, half), sds(total, half), sds(total, half),
             ),
             in_specs=[vmem, vmem, hbm, hbm, hbm],
-            out_specs=(vmem, vmem, hbm, hbm, hbm, hbm, hbm, hbm),
+            out_specs=(hbm, hbm, hbm, hbm, hbm, hbm, hbm, hbm),
             scratch_shapes=[
                 buf(feats, half), buf(feats, half), buf(half, feats),
                 buf(total, feats), buf(total, feats),
                 buf(nz, 3, 2 * tl, half), buf(nz, 3, 3, tl // 2, half),
                 buf(3, total, half), pltpu.VMEM((2, 2 * tl, feats), F32),
                 buf(nz, 2, 2, tl, feats), buf(nz, 2, tl, feats), buf(nz, 2, tl, feats),
-                buf(nz - 2, 2, tl, feats),
+                buf(nz - 2, 2, tl, feats), pltpu.VMEM((2, tl, feats), F32),
                 sem(3, 2), sem(2), sem(2 * nz, 3),
                 sem(nz, 3), sem(nz * 2), sem(nz, 3), sem(nz * 2),
                 sem(2 * nz, 2, 5), sem(2 * nz, 2, 5), sem(2 * nz, 4), sem(2 * nz, 4),
-                sem(nz), sem(nz), sem(nz), sem(nz), pltpu.SemaphoreType.DMA,
+                sem(nz), sem(nz), sem(nz), sem(nz), pltpu.SemaphoreType.DMA, sem(2),
             ],
             compiler_params=pltpu.CompilerParams(
                 collective_id=1, has_side_effects=True, vmem_limit_bytes=60 * 2**20

time: 137 us -> 135 us (0.985)
  Pallas kernels: 135 us -> 133 us
where the time goes in v5:
time: 135 us
  Pallas kernels  133 us (99%)
    pallas_call x1, Pallas kernels, per_device(): pl.pallas_call(functools.partial(group_kernel, (nz, tl, half, 2 * pw if p...  116 us
    pallas_call x1, Pallas kernels, weight_grads(): pl.pallas_call(weight_kernel, in_specs=[hbm] * 5, out_specs=(hbm, hbm, hb...  17.1 us
  transfers between devices with their start and end apart: 1, of which 0 were waited for; matrix products, arithmetic and copies ran while one was open for 0% of the time, Pallas kernels for 13%

profile of v5, /device:TPU:0, one launch (start us, length us, event | category | flops | bytes accessed | tf_op | source)
XLA Modules:
  0.0 135.2 jit_solution(380138605102343246)
XLA Ops:
  0.6 116.3 %shard_map.92 = (f32[64,2048]{1,0:T(8,128)}, f32[64,2048]{1,0:T(8,128)}, bf16[2,64,2048]{2,1,0:T(8,128)(2,1)}, bf16[512,2048]{1,0:T(8,128)(2,1)}, bf16[512,2048]...) custom-call(bf16[64,2048]{1,0:T(8,128)(2,1)} %x_ref.1, ...), custom_call_target="tpu_custom_call" | custom-call | flops 22548578304 | bytes 29360128 | tf_op jit(solution)/shard_map/pallas_call | solution.py:878
  116.9 0.2 collective-permute-start
  117.2 0.0 copy-start
  117.2 0.0 copy-start.1
  117.2 17.1 %shard_map.93 = (bf16[2048,1792]{1,0:T(8,128)(2,1)}, bf16[2048,1792]{1,0:T(8,128)(2,1)}, bf16[1792,2048]{1,0:T(8,128)(2,1)}) custom-call(bf16[512,2048]{1,0:T(8,128)(2,1)} %get-tuple-element.19.x_hbm, bf16[512,1792]{1,0:T(8,128)(2,1)} %get-tuple-element.20.dg_hbm, bf16[512,1792]{1,0:T(8,128)(2,1)} %get-tuple-element.21.du_hbm, ...), custom_call_target="tpu_custom_call" | custom-call | flops 11274289152 | bytes 31719424 | tf_op jit(solution)/shard_map/pallas_call | solution.py:823
  134.3 0.0 collective-permute-done
  134.3 0.0 copy-done
  134.3 0.0 copy-done.1
  134.3 0.9 fusion
Async XLA Ops:
  116.9 17.4 %collective-permute-start = (bf16[2,64,2048]{2,1,0:T(8,128)(2,1)}, bf16[2,64,2048]{2,1,0:T(8,128)(2,1)S(1)}, u32[]{:S(2)}, u32[]{:S(2)}) collective-permute-start(bf16[2,64,2048]{2,1,0:T(8,128)(2,1)} %get-tuple-element.17), channel_id=1, source_target_pairs={{0,2},{2,4},{4,6},{6,0},{1,3},{3,5},{5,7},{7,1},{8,10},{10,12},{12... | collective-permute-start | bytes 1572872 | tf_op jit(solution)/shard_map/ppermute | solution.py:908
  117.2 17.2 %copy-start = (f32[64,2048]{1,0:T(8,128)S(1)}, f32[64,2048]{1,0:T(8,128)}, u32[]{:S(2)}) copy-start(f32[64,2048]{1,0:T(8,128)} %get-tuple-element.16) | copy-start | bytes 1572868
  117.2 17.2 %copy-start.1 = (f32[64,2048]{1,0:T(8,128)S(1)}, f32[64,2048]{1,0:T(8,128)}, u32[]{:S(2)}) copy-start(f32[64,2048]{1,0:T(8,128)} %get-tuple-element.18) | copy-start | bytes 1572868

commit v6 on v5

--- a/solution.py
+++ b/solution.py
@@ -511,9 +511,10 @@
         to = (p, q, q, p)[m]
         return remote(ref, ref, ag_ssem.at[u, m], ag_rsem.at[u, m], {"row": to})
 
-    def to_sibling(i):
-        g = group(i)
-        return remote(s_part.at[g, :, 1 - d], s_sib.at[g], sib_ssem.at[i], sib_rsem.at[i], sibling)
+    def to_sibling(i, p):
+        g, cols = group(i), block(p, pw)
+        return remote(s_part.at[g, :, 1 - d, :, cols], s_sib.at[g, :, :, cols],
+                      sib_ssem.at[i, p], sib_rsem.at[i, p], sibling)
 
     def to_col(i):
         g = group(i)
@@ -651,14 +652,17 @@
                     value = (value + acc[j, :, cols]).astype(BF16)
                     for dd in range(2):
                         s_part[g, j, dd, :, cols] = value[dd * tl:(dd + 1) * tl]
-
-            to_sibling(i).start()
+                to_sibling(i, p).start()
 
     def spread(i):
         g = group(i)
-        to_sibling(i).wait_recv()
-        for j in range(2):
-            s_sum[g, j] = (s_part[g, j, d].astype(F32) + s_sib[g, j].astype(F32)).astype(BF16)
+        for p in range(feats // pw):
+            to_sibling(i, p).wait_recv()
+            cols = pl.ds(p * pw, pw)
+            for j in range(2):
+                s_sum[g, j, :, cols] = (
+                    s_part[g, j, d, :, cols].astype(F32) + s_sib[g, j, :, cols].astype(F32)
+                ).astype(BF16)
 
 
         @pl.when((i > 0) & (i < nz - 1))
@@ -755,7 +759,8 @@
     to_last = pltpu.make_async_copy(s_sum.at[group(nz - 1)], last_ref, last_sem)
     to_last.start()
     for i in range(nz):
-        to_sibling(i).wait_send()
+        for p in range(feats // pw):
+            to_sibling(i, p).wait_send()
     x_save.wait()
     cot_save.wait()
     for copy in to_base:
@@ -769,23 +774,26 @@
 ):
     halves = []
     for k, (src, dst) in enumerate(((x_hbm, x), (dg_hbm, dg), (du_hbm, du), (act_hbm, act), (cot_hbm, cot))):
-        width = src.shape[1] // 2
+        width = (src.shape[1] // 2 + 255) // 256 * 256
         halves.append([
             pltpu.make_async_copy(src.at[:, cols], dst.at[:, cols], in_sem.at[k, c])
-            for c, cols in enumerate((pl.ds(0, width), pl.ds(width, width)))
+            for c, cols in enumerate((pl.ds(0, width), pl.ds(width, src.shape[1] - width)))
         ])
 
+    def spans(ref, cut):
+        return pl.ds(0, cut), pl.ds(cut, ref.shape[1] - cut)
+
     def product(k, left, right, tile, result, before):
-        rows, width = left.shape[1] // 2, right.shape[1] // 2
+        rows, width = ((ref.shape[1] // 2 + 255) // 256 * 256 for ref in (left, right))
         saves = []
         for i in range(2):
             for c in range(2):
                 for step in before.pop((i, c), ()):
                     step()
-                here, cols = pl.ds(i * rows, rows), pl.ds(c * width, width)
-                tile[i, :, cols] = dot_tn(left[:, here], right[:, cols]).astype(BF16)
+                here, cols = spans(left, rows)[i], spans(right, width)[c]
+                tile[i, :spans(left, rows)[i].size, cols] = dot_tn(left[:, here], right[:, cols]).astype(BF16)
                 save = pltpu.make_async_copy(
-                    tile.at[i, :, cols], result.at[here, cols], out_sem.at[k, i, c])
+                    tile.at[i, :spans(left, rows)[i].size, cols], result.at[here, cols], out_sem.at[k, i, c])
                 save.start()
                 saves.append(save)
         return saves
@@ -814,7 +822,7 @@
 def weight_grads(x, dgate, dup, act, cot):
     total, feats = x.shape
     half = act.shape[1]
-    tall, short = feats // 2, half // 2
+    tall, short = ((size // 2 + 255) // 256 * 256 for size in (feats, half))
     hbm = pl.BlockSpec(memory_space=pl.ANY)
 
     def buf(*shape):
@@ -895,7 +903,7 @@
                 sem(3, 2), sem(2), sem(2 * nz, 3),
                 sem(nz, 3), sem(nz * 2), sem(nz, 3), sem(nz * 2),
                 sem(2 * nz, 2, 5), sem(2 * nz, 2, 5), sem(2 * nz, 4), sem(2 * nz, 4),
-                sem(nz), sem(nz), sem(nz), sem(nz), pltpu.SemaphoreType.DMA, sem(2),
+                sem(nz, parts), sem(nz, parts), sem(nz), sem(nz), pltpu.SemaphoreType.DMA, sem(2),
             ],
             compiler_params=pltpu.CompilerParams(
                 collective_id=1, has_side_effects=True, vmem_limit_bytes=60 * 2**20

time: 135 us -> 135 us (level)
  transfers between devices with their start and end apart: 1 -> 1, of which waited for: 0 -> 0; matrix products, arithmetic and copies ran while one was open for 0% -> 0% of each run, Pallas kernels for 13% -> 12%
where the time goes in v6:
time: 135 us
  Pallas kernels  132 us (98%)
    pallas_call x1, Pallas kernels, per_device(): pl.pallas_call(functools.partial(group_kernel, (nz, tl, half, 2 * pw if p...  116 us
    pallas_call x1, Pallas kernels, weight_grads(): pl.pallas_call(weight_kernel, in_specs=[hbm] * 5, out_specs=(hbm, hbm, hb...  16.6 us
  transfers between devices with their start and end apart: 1, of which 0 were waited for; matrix products, arithmetic and copies ran while one was open for 0% of the time, Pallas kernels for 12%

profile of v6, /device:TPU:0, one launch (start us, length us, event | category | flops | bytes accessed | tf_op | source)
XLA Modules:
  0.0 134.6 jit_solution(4461670870192602299)
XLA Ops:
  0.6 115.7 %shard_map.92 = (f32[64,2048]{1,0:T(8,128)}, f32[64,2048]{1,0:T(8,128)}, bf16[2,64,2048]{2,1,0:T(8,128)(2,1)}, bf16[512,2048]{1,0:T(8,128)(2,1)}, bf16[512,2048]...) custom-call(bf16[64,2048]{1,0:T(8,128)(2,1)} %x_ref.1, ...), custom_call_target="tpu_custom_call" | custom-call | flops 22548578304 | bytes 29360128 | tf_op jit(solution)/shard_map/pallas_call | solution.py:886
  116.3 0.7 collective-permute-start
  117.0 0.0 copy-start
  117.0 0.0 copy-start.1
  117.0 16.6 %shard_map.93 = (bf16[2048,1792]{1,0:T(8,128)(2,1)}, bf16[2048,1792]{1,0:T(8,128)(2,1)}, bf16[1792,2048]{1,0:T(8,128)(2,1)}) custom-call(bf16[512,2048]{1,0:T(8,128)(2,1)} %get-tuple-element.19.x_hbm, bf16[512,1792]{1,0:T(8,128)(2,1)} %get-tuple-element.20.dg_hbm, bf16[512,1792]{1,0:T(8,128)(2,1)} %get-tuple-element.21.du_hbm, ...), custom_call_target="tpu_custom_call" | custom-call | flops 11274289152 | bytes 31719424 | tf_op jit(solution)/shard_map/pallas_call | solution.py:831
  133.7 0.0 collective-permute-done
  133.7 0.0 copy-done
  133.7 0.0 copy-done.1
  133.7 0.9 fusion
Async XLA Ops:
  116.3 17.3 %collective-permute-start = (bf16[2,64,2048]{2,1,0:T(8,128)(2,1)}, bf16[2,64,2048]{2,1,0:T(8,128)(2,1)S(1)}, u32[]{:S(2)}, u32[]{:S(2)}) collective-permute-start(bf16[2,64,2048]{2,1,0:T(8,128)(2,1)} %get-tuple-element.17), channel_id=1, source_target_pairs={{0,2},{2,4},{4,6},{6,0},{1,3},{3,5},{5,7},{7,1},{8,10},{10,12},{12... | collective-permute-start | bytes 1572872 | tf_op jit(solution)/shard_map/ppermute | solution.py:916
  117.0 16.7 %copy-start = (f32[64,2048]{1,0:T(8,128)S(1)}, f32[64,2048]{1,0:T(8,128)}, u32[]{:S(2)}) copy-start(f32[64,2048]{1,0:T(8,128)} %get-tuple-element.16) | copy-start | bytes 1572868
  117.0 16.7 %copy-start.1 = (f32[64,2048]{1,0:T(8,128)S(1)}, f32[64,2048]{1,0:T(8,128)}, u32[]{:S(2)}) copy-start(f32[64,2048]{1,0:T(8,128)} %get-tuple-element.18) | copy-start | bytes 1572868

commit v7 on v6

--- a/solution.py
+++ b/solution.py
@@ -393,7 +393,7 @@
         )[i]
         return pltpu.make_async_copy(src, dst, w_sem.at[i, s])
 
-    for i in range(3):
+    for i in range(2):
         load(i, 0).start()
 
     def remote(src, dst, ssem, rsem, where):
@@ -681,6 +681,7 @@
     pl.semaphore_wait(barrier, 2 + nz - 1 + 1)
     x_first(x_ref)
     c_first(cot_ref)
+    load(2, 0).start()
 
     @pl.loop(0, units + 3)
     def _(t):

time: 135 us -> 135 us (level)
  no operation moved by 1% of the time
where the time goes in v7:
time: 135 us
  Pallas kernels  132 us (98%)
    pallas_call x1, Pallas kernels, per_device(): pl.pallas_call(functools.partial(group_kernel, (nz, tl, half, 2 * pw if p...  116 us
    pallas_call x1, Pallas kernels, weight_grads(): pl.pallas_call(weight_kernel, in_specs=[hbm] * 5, out_specs=(hbm, hbm, hb...  16.6 us
  transfers between devices with their start and end apart: 1, of which 0 were waited for; matrix products, arithmetic and copies ran while one was open for 0% of the time, Pallas kernels for 12%

profile of v7, /device:TPU:0, one launch (start us, length us, event | category | flops | bytes accessed | tf_op | source)
XLA Modules:
  0.0 134.6 jit_solution(12536732994635227566)
XLA Ops:
  0.6 115.7 %shard_map.92 = (f32[64,2048]{1,0:T(8,128)}, f32[64,2048]{1,0:T(8,128)}, bf16[2,64,2048]{2,1,0:T(8,128)(2,1)}, bf16[512,2048]{1,0:T(8,128)(2,1)}, bf16[512,2048]...) custom-call(bf16[64,2048]{1,0:T(8,128)(2,1)} %x_ref.1, ...), custom_call_target="tpu_custom_call" | custom-call | flops 22548578304 | bytes 29360128 | tf_op jit(solution)/shard_map/pallas_call | solution.py:887
  116.3 0.7 collective-permute-start
  117.0 0.0 copy-start
  117.0 0.0 copy-start.1
  117.0 16.6 %shard_map.93 = (bf16[2048,1792]{1,0:T(8,128)(2,1)}, bf16[2048,1792]{1,0:T(8,128)(2,1)}, bf16[1792,2048]{1,0:T(8,128)(2,1)}) custom-call(bf16[512,2048]{1,0:T(8,128)(2,1)} %get-tuple-element.19.x_hbm, bf16[512,1792]{1,0:T(8,128)(2,1)} %get-tuple-element.20.dg_hbm, bf16[512,1792]{1,0:T(8,128)(2,1)} %get-tuple-element.21.du_hbm, ...), custom_call_target="tpu_custom_call" | custom-call | flops 11274289152 | bytes 31719424 | tf_op jit(solution)/shard_map/pallas_call | solution.py:832
  133.7 0.0 collective-permute-done
  133.7 0.0 copy-done
  133.7 0.0 copy-done.1
  133.7 0.9 fusion
Async XLA Ops:
  116.3 17.3 %collective-permute-start = (bf16[2,64,2048]{2,1,0:T(8,128)(2,1)}, bf16[2,64,2048]{2,1,0:T(8,128)(2,1)S(1)}, u32[]{:S(2)}, u32[]{:S(2)}) collective-permute-start(bf16[2,64,2048]{2,1,0:T(8,128)(2,1)} %get-tuple-element.17), channel_id=1, source_target_pairs={{0,2},{2,4},{4,6},{6,0},{1,3},{3,5},{5,7},{7,1},{8,10},{10,12},{12... | collective-permute-start | bytes 1572872 | tf_op jit(solution)/shard_map/ppermute | solution.py:917
  117.0 16.7 %copy-start = (f32[64,2048]{1,0:T(8,128)S(1)}, f32[64,2048]{1,0:T(8,128)}, u32[]{:S(2)}) copy-start(f32[64,2048]{1,0:T(8,128)} %get-tuple-element.16) | copy-start | bytes 1572868
  117.0 16.7 %copy-start.1 = (f32[64,2048]{1,0:T(8,128)S(1)}, f32[64,2048]{1,0:T(8,128)}, u32[]{:S(2)}) copy-start(f32[64,2048]{1,0:T(8,128)} %get-tuple-element.18) | copy-start | bytes 1572868
